TPU v7x, 128 devices: a whole 4x4x4 slice. The times are simulated.
128 devices in a mesh: shot: 16 (over y, z), recv: 8 (over x, core).
Axes of the slice: x: 4, y: 4, z: 4, core: 2. Of those that a mesh axis runs over, the one named last changes fastest.
Arguments:
- shot_feats: bfloat16 [64, 64, 256, 384], P(None, 'shot', 'recv'), may hold values from -40 to 40
- norm_gain: float32 [64], replicated, may hold values from 0.25 to 1.75
- shot_taps: float32 [2, 2, 64, 5], replicated, may hold values from -3 to 3
- shot_mix: bfloat16 [2, 64, 64], replicated, may hold values from -0.75 to 0.75
- shot_bias: float32 [2, 64], replicated, may hold values from -0.5 to 0.5
- recv_taps: float32 [2, 2, 64, 5], replicated, may hold values from -3 to 3
- recv_mix: bfloat16 [2, 64, 64], replicated, may hold values from -0.75 to 0.75
- recv_bias: float32 [2, 64], replicated, may hold values from -0.5 to 0.5
- pack_index: int32 [2048, 12], P(('shot', 'recv')), may hold values from -1 to 127, as said below
- recv_index: int32 [1024, 24], P(('shot', 'recv')), may hold values from -1 to 191, as said below
Outputs:
- recv_feats: bfloat16 [64, 1024, 24, 384], P(None, ('shot', 'recv'))
Inputs may be any that keep to these rules, and one draw needn't show every extreme that they name: `pack_index`: on each device's 16 rows every local trace (local shot * 32 + trace within the tile) is named exactly once; live slots of a row come first, the rest are -1; on every device some row has all 12 slots live. `recv_index`: within receiver block d of tile j every live slot c of row d of the pack_index rows of each shot block s of tile j is named exactly once, as s * 12 + c, and nothing else is named; a receiver's live slots come first and are ordered by shot, then trace; each receiver has from 8 to 24 live slots, and every block has a receiver with all 24 live.
All inputs are finite; a program needn't handle non-finite values.
Results may differ from a plain program's by a relative error of at most 0.015.
Values may be sent and summed in bfloat16 or wider, within the bound.
No kernel may reach another device: no remote copies, remote signals or barrier semaphores. Data moves between devices by JAX's collectives and lax.ppermute only.
A program may use at most 128 MiB of HBM per device.

v0:
```python
import jax
import jax.numpy as jnp
from jax import lax
from jax.sharding import PartitionSpec as P

TRACES = 256
LAYERS = 2


def padded_2(block, sides, width):
    for axis, dim in sides:
        count = lax.axis_size(axis)
        forward = [(i, i + 1) for i in range(count - 1)]
        backward = [(target, source) for source, target in forward]
        low = lax.ppermute(
            lax.slice_in_dim(block, block.shape[dim] - width, None, axis=dim), axis, forward
        )
        high = lax.ppermute(lax.slice_in_dim(block, 0, width, axis=dim), axis, backward)
        block = jnp.concatenate([low, block, high], axis=dim)
    return block


def dilated(padded, kernel, axis_index, length):
    target = (kernel.shape[0],) + (1,) * (padded.ndim - 1)
    summed = kernel[:, 0].reshape(target) * lax.slice_in_dim(padded, 0, length, axis=axis_index)
    for offset in range(1, 5):
        summed = summed + kernel[:, offset].reshape(target) * lax.slice_in_dim(
            padded, 2 * offset, 2 * offset + length, axis=axis_index
        )
    return summed


def zero_conv(values, kernel, axis_index):
    widths = [(0, 0)] * values.ndim
    widths[axis_index] = (4, 4)
    return dilated(jnp.pad(values, widths), kernel, axis_index, values.shape[axis_index])


def mixing(inputs, weight, bias_row):
    product = jnp.einsum("oc,cabd->oabd", weight, inputs, preferred_element_type=jnp.float32)
    return jax.nn.relu(product + bias_row[:, None, None, None])


def stencil(current, kernel_pair, scaled_by):
    padded = padded_2(current, (("recv", 2),), 4)
    traces_here = current.shape[2]
    if scaled_by is None:
        across = dilated(padded, kernel_pair[0], 2, traces_here)
        return zero_conv(across, kernel_pair[1], 3).astype(jnp.bfloat16)
    across = dilated(padded.astype(jnp.float32) * scaled_by, kernel_pair[0], 2, traces_here)
    return zero_conv(across, kernel_pair[1], 3).astype(jnp.bfloat16)


def per_device(
    shot_feats,
    norm_gain,
    shot_taps,
    shot_mix,
    shot_bias,
    recv_taps,
    recv_mix,
    recv_bias,
    pack_index,
    recv_index,
):
    channels, shots_here, traces_here, samples = shot_feats.shape
    energy = lax.psum(jnp.sum(jnp.square(shot_feats.astype(jnp.float32)), axis=(0, 2, 3)), "recv")
    shot_rms = jnp.sqrt(energy / (channels * TRACES * samples) + 1e-05)
    scaled_by = norm_gain[:, None, None, None] / shot_rms[None, :, None, None]
    current = shot_feats
    depth = 0
    mixed_in = stencil(current, shot_taps[depth], scaled_by)
    current = mixing(mixed_in, shot_mix[depth], shot_bias[depth]).astype(jnp.bfloat16)
    last_in = stencil(current, shot_taps[LAYERS - 1], None)
    blocks, capacity = pack_index.shape
    rows_here, fold_slots = recv_index.shape
    send_index = pack_index.reshape(-1)
    send_live = (send_index >= 0)[None, :, None]
    keep_index = recv_index.reshape(-1)
    keep_live = (keep_index >= 0)[None, :, None]
    last_out = mixing(last_in, shot_mix[LAYERS - 1], shot_bias[LAYERS - 1]).astype(jnp.bfloat16)
    flattened = last_out.reshape(channels, shots_here * traces_here, samples)
    picked = jnp.take(flattened, jnp.maximum(send_index, 0), axis=1)
    picked = jnp.where(send_live, picked, jnp.zeros((), picked.dtype))
    buffer = lax.all_to_all(
        picked.reshape(channels, blocks, capacity, samples),
        "shot",
        split_axis=1,
        concat_axis=1,
        tiled=True,
    )
    items_here = buffer.shape[0]
    flattened = buffer.reshape(items_here, -1, samples)
    unpack_picked = jnp.take(flattened, jnp.maximum(keep_index, 0), axis=1)
    unpack_picked = jnp.where(keep_live, unpack_picked, jnp.zeros((), unpack_picked.dtype))
    regrouped = unpack_picked.reshape(items_here, rows_here, fold_slots, samples)
    live_mask = (recv_index >= 0).astype(jnp.float32)[None, :, :, None]
    for depth in range(LAYERS):
        across = zero_conv(regrouped, recv_taps[depth, 0], 2)
        mixed_in = zero_conv(across, recv_taps[depth, 1], 3).astype(jnp.bfloat16)
        regrouped = (mixing(mixed_in, recv_mix[depth], recv_bias[depth]) * live_mask).astype(
            jnp.bfloat16
        )
    return regrouped


def solution(mesh):
    return jax.shard_map(
        per_device,
        mesh=mesh,
        in_specs=(
            P(None, "shot", "recv", None),
            P(),
            P(),
            P(),
            P(),
            P(),
            P(),
            P(),
            P(("shot", "recv"), None),
            P(("shot", "recv"), None),
        ),
        out_specs=P(None, ("shot", "recv"), None, None),
        check_vma=False,
    )
```

profile of v0, /device:TPU:85, one launch (start us, length us, event | category | flops | bytes accessed | tf_op | source)
XLA Modules:
  0.0 530.8 jit_solution(15992591127748317216)
XLA Ops:
  0.0 0.0 copy-start.7
  0.0 2.6 fusion.74
  2.6 0.2 copy.49
  2.8 3.4 collective-permute-start
  6.2 0.2 copy.50
  6.3 1.9 collective-permute-start.1
  8.3 4.5 multiply_reduce_fusion
  12.8 0.0 copy-done.3
  12.8 12.0 %psum.7 = f32[4]{0:T(128)S(1)} all-reduce(f32[4]{0:T(128)S(1)} %multiply_reduce_fusion), channel_id=1, replica_groups=mesh['shot'=16,'recv'=8] {'recv'}, use_global_device_ids=true, to_apply=%region_1.0 | all-reduce | flops 4 | bytes 32 | tf_op jit(solution)/shard_map/psum | solution.py:67
  24.8 0.0 copy-done.5
  24.8 0.0 copy-done.1
  24.9 0.0 copy-done.7
  24.9 0.1 broadcast_divide_fusion
  24.9 0.0 collective-permute-done
  25.0 0.6 copy.33
  25.6 0.0 collective-permute-done.1
  25.6 0.6 copy.34
  26.2 9.5 %convert_multiply_fusion = f32[64,4,40,384]{3,2,1,0:T(8,128)} fusion(bf16[64,4,4,384]{3,2,1,0:T(4,128)(2,1)S(1)} %copy.34, bf16[64,4,32,384]{3,2,1,0:T(8,128)(2,1)} %param.10, bf16[64,4,4,384]{3,2,1,0:T(4,128)(2,1)S(1)} %copy.33, f32[64,4]{1,0:T(8,128)S(1)} %broadcast_divide_fusion), kind=kLoop, calls=%fused_computation.40 | loop fusion | flops 27525120 | bytes 23593984 | tf_op jit(solution)/shard_map/mul | solution.py:50
  35.7 29.8 %fusion.36 = f32[64,4,32,384]{3,2,1,0:T(8,128)} fusion(f32[64,4,40,384]{3,2,1,0:T(8,128)} %convert_multiply_fusion, f32[64]{0:T(128)S(1)} %get-tuple-element.58, f32[64]{0:T(128)S(1)} %get-tuple-element.59, f32[64]{0:T(128)S(1)} %get-tuple-element.60, f32[64]{0:T(128)S(1)} %get-tuple-element.61, f32[64]{0:T(128)S(1)} %get-tuple-element.57), kind=kLoop, calls=%fused_computation.68 | loop fusion | flops 28311552 | bytes 75498752 | tf_op jit(solution)/shard_map/add | solution.py:27
  65.5 31.8 %fusion.23 = bf16[64,4,32,384]{3,2,1,0:T(8,128)(2,1)S(1)} fusion(f32[64,4,32,384]{3,2,1,0:T(8,128)} %fusion.36, f32[64]{0:T(128)S(1)} %get-tuple-element.53, f32[64]{0:T(128)S(1)} %get-tuple-element.54, f32[64]{0:T(128)S(1)} %get-tuple-element.55, f32[64]{0:T(128)S(1)} %get-tuple-element.56, f32[64]{0:T(128)S(1)} %get-tuple-element.52), kind=kLoop, calls=%fused_computation.54 | loop fusion | flops 31457280 | bytes 18875648 | tf_op jit(solution)/shard_map/convert_element_type | solution.py:51
  97.3 0.0 copy-done.8
  97.3 7.0 %fusion.48 = bf16[64,4,32,384]{3,0,2,1:T(8,128)(2,1)S(1)} fusion(f32[64]{0:T(128)S(1)} %get-tuple-element.62, bf16[64,4,32,384]{3,2,1,0:T(8,128)(2,1)S(1)} %fusion.23, bf16[2,64,64]{2,1,0:T(8,128)(2,1)S(1)} %copy-done.8), kind=kOutput, calls=%fused_computation.92 | convolution fusion | flops 412090368 | bytes 12599808 | tf_op jit(solution)/shard_map/oc,cabd->oabd/dot_general | solution.py:40
  104.3 0.0 copy-start
  104.3 2.7 copy-done
  107.0 0.2 fusion.73
  107.2 4.2 collective-permute-start.2
  111.4 2.1 collective-permute-start.3
  113.5 0.1 reshape.151
  113.7 6.6 %collective-permute-done.2 = bf16[64,4,4,384]{3,0,2,1:T(8,128)(2,1)S(1)} collective-permute-done((bf16[64,4,4,384]{3,0,2,1:T(8,128)(2,1)S(1)}, bf16[64,4,4,384]{3,0,2,1:T(8,128)(2,1)S(1)}, u32[]{:S(2)}, u32[]{:S(2)}) %collective-permute-start.2) | collective-permute-done | bytes 786464 | tf_op jit(solution)/shard_map/ppermute | solution.py:15
  120.3 4.4 collective-permute-done.3
  124.7 17.7 %multiply_add_fusion.2 = f32[64,4,32,384]{3,0,2,1:T(8,128)} fusion(bf16[64,4,32,384]{3,0,2,1:T(8,128)(2,1)} %copy-done, bf16[64,4,4,384]{3,0,2,1:T(8,128)(2,1)S(1)} %collective-permute-done.3, bf16[64,4,4,384]{3,0,2,1:T(8,128)(2,1)S(1)} %collective-permute-done.2, f32[64]{0:T(128)S(1)} %get-tuple-element.48, f32[64]{0:T(128)S(1)} %get-tuple-element.49, ...), kind=kLoop, calls=%fused_computation.77 | loop fusion | flops 56623104 | bytes 20448512 | tf_op jit(solution)/shard_map/add | solution.py:27
  142.4 33.0 %maximum_convert_fusion = bf16[4,32,384,64]{2,3,1,0:T(8,128)(2,1)} fusion(f32[64]{0:T(128)S(1)} %get-tuple-element.63, f32[64,4,32,384]{3,0,2,1:T(8,128)} %multiply_add_fusion.2, f32[64]{0:T(128)S(1)} %get-tuple-element.43, f32[64]{0:T(128)S(1)} %get-tuple-element.44, f32[64]{0:T(128)S(1)} %get-tuple-element.45, f32[64]{0:T(128)S(1)} %get-tuple-element.46, ...), kind=kOutput, calls=%fused_computation.76 | convolution fusion | flops 443547648 | bytes 18893824 | tf_op jit(solution)/shard_map/oc,cabd->oabd/dot_general | solution.py:40
  175.4 12.9 %gather_fusion = bf16[192,64,384]{2,1,0:T(8,128)(2,1)} fusion(bf16[64,128,384]{2,0,1:T(8,128)(2,1)} %bitcast.160, s32[1024]{0:T(1024)S(1)} %pad_clamp_fusion.1), kind=kCustom, calls=%fused_computation | custom fusion | bytes 18875136 | tf_op jit(solution)/shard_map/jit(_take)/gather | solution.py:83
  188.4 8.9 %select_select_fusion.1 = bf16[64,16,12,384]{3,0,2,1:T(8,128)(2,1)} fusion(bf16[64,16,12,384]{3,0,2,1:T(8,128)(2,1)} %bitcast.158, pred[16,12]{1,0:T(8,128)(4,1)S(1)} %get-tuple-element.20, pred[16,12]{1,0:T(8,128)(4,1)S(1)} %get-tuple-element.19), kind=kLoop, calls=%fused_computation.83 | loop fusion | flops 9437184 | bytes 18874752 | tf_op jit(solution)/shard_map/jit(_where)/select_n | solution.py:84
  197.3 7.5 %all-to-all-start = ((bf16[64,16,12,384]{3,0,2,1:T(8,128)(2,1)}), bf16[64,16,12,384]{3,0,2,1:T(8,128)(2,1)}, u32[]{:S(2)}, u32[]{:S(2)}) async-start(bf16[64,16,12,384]{3,0,2,1:T(8,128)(2,1)} %select_select_fusion.1), calls=%async_computation | async-start | bytes 18874368 | tf_op jit(solution)/shard_map/all_to_all | solution.py:85
  204.8 0.0 copy-done.2
  204.8 0.1 reshape.159
  204.9 0.0 copy-done.6
  204.9 0.0 copy-done.4
  205.0 169.6 %all-to-all-done = bf16[64,16,12,384]{3,0,2,1:T(8,128)(2,1)} async-done(((bf16[64,16,12,384]{3,0,2,1:T(8,128)(2,1)}), bf16[64,16,12,384]{3,0,2,1:T(8,128)(2,1)}, u32[]{:S(2)}, u32[]{:S(2)}) %all-to-all-start) | async-done | bytes 9437216 | tf_op jit(solution)/shard_map/all_to_all | solution.py:85
  374.7 13.8 %gather_fusion.1 = bf16[192,64,384]{2,1,0:T(8,128)(2,1)} fusion(bf16[64,192,384]{2,0,1:T(8,128)(2,1)} %bitcast.45, s32[1024]{0:T(1024)S(1)} %pad_clamp_fusion), kind=kCustom, calls=%fused_computation.1 | custom fusion | bytes 18875136 | tf_op jit(solution)/shard_map/jit(_take)/gather | solution.py:94
  388.5 8.9 %select_select_fusion = bf16[64,8,24,384]{3,0,2,1:T(8,128)(2,1)} fusion(bf16[64,8,24,384]{3,0,2,1:T(8,128)(2,1)} %bitcast.159, pred[8,24]{1,0:T(8,128)(4,1)S(1)} %get-tuple-element.41, pred[8,24]{1,0:T(8,128)(4,1)S(1)} %get-tuple-element.6), kind=kLoop, calls=%fused_computation.82 | loop fusion | flops 9437184 | bytes 18874752 | tf_op jit(solution)/shard_map/jit(_where)/select_n | solution.py:95
  397.4 23.3 %multiply_add_fusion.1 = f32[64,8,24,384]{3,0,2,1:T(8,128)} fusion(bf16[64,8,24,384]{3,0,2,1:T(8,128)(2,1)} %select_select_fusion, f32[64]{0:T(128)S(1)} %get-tuple-element.37, f32[64]{0:T(128)S(1)} %get-tuple-element.38, f32[64]{0:T(128)S(1)} %get-tuple-element.39, f32[64]{0:T(128)S(1)} %get-tuple-element.40, f32[64]{0:T(128)S(1)} %get-tuple-element.36), kind=kLoop, calls=%fused_computation.39 | loop fusion | flops 66060288 | bytes 28312832 | tf_op jit(solution)/shard_map/add | solution.py:27
  420.7 0.0 copy-done.9
  420.7 36.7 %fusion.40 = bf16[64,8,24,384]{3,0,2,1:T(8,128)(2,1)} fusion(f32[8,24]{1,0:T(8,128)S(1)} %get-tuple-element.5, f32[64]{0:T(128)S(1)} %get-tuple-element.64, f32[64,8,24,384]{3,0,2,1:T(8,128)} %multiply_add_fusion.1, f32[64]{0:T(128)S(1)} %get-tuple-element.32, f32[64]{0:T(128)S(1)} %get-tuple-element.33, f32[64]{0:T(128)S(1)} %get-tuple-element.34, ...), kind=kOutput, calls=%fused_computation.80 | convolution fusion | flops 670040064 | bytes 28335104 | tf_op jit(solution)/shard_map/oc,cabd->oabd/dot_general | solution.py:40
  457.4 23.3 %multiply_add_fusion = f32[64,8,24,384]{3,0,2,1:T(8,128)} fusion(bf16[64,8,24,384]{3,0,2,1:T(8,128)(2,1)} %fusion.40, f32[64]{0:T(128)S(1)} %get-tuple-element.27, f32[64]{0:T(128)S(1)} %get-tuple-element.28, f32[64]{0:T(128)S(1)} %get-tuple-element.29, f32[64]{0:T(128)S(1)} %get-tuple-element.30, f32[64]{0:T(128)S(1)} %get-tuple-element.26), kind=kLoop, calls=%fused_computation.37 | loop fusion | flops 66060288 | bytes 28312832 | tf_op jit(solution)/shard_map/add | solution.py:27
  480.7 36.9 %fusion.41 = bf16[64,8,24,384]{3,0,2,1:T(8,128)(2,1)} fusion(f32[64]{0:T(128)S(1)} %get-tuple-element.65, f32[8,24]{1,0:T(8,128)S(1)} %get-tuple-element.5, f32[64,8,24,384]{3,0,2,1:T(8,128)} %multiply_add_fusion, f32[64]{0:T(128)S(1)} %get-tuple-element.22, f32[64]{0:T(128)S(1)} %get-tuple-element.23, f32[64]{0:T(128)S(1)} %get-tuple-element.24, ...), kind=kOutput, calls=%fused_computation.81 | convolution fusion | flops 670040064 | bytes 28335104 | tf_op jit(solution)/shard_map/oc,cabd->oabd/dot_general | solution.py:40
  517.6 13.0 %copy.36 = bf16[64,8,24,384]{3,2,1,0:T(8,128)(2,1)} copy(bf16[64,8,24,384]{3,0,2,1:T(8,128)(2,1)} %fusion.41) | data formatting | bytes 18874368 | tf_op jit(solution)/shard_map/convert_element_type | solution.py:101
  (31 shorter events, 0.1 us)
Async XLA Ops:
  0.0 12.8 %copy-start.3 = (f32[2,2,64,5]{2,1,3,0:T(2,128)S(1)}, f32[2,2,64,5]{2,1,3,0:T(2,128)}, u32[]{:S(2)}) copy-start(f32[2,2,64,5]{2,1,3,0:T(2,128)} %param.12) | copy-start | bytes 15364
  0.0 24.8 %copy-start.5 = (f32[2,64]{1,0:T(2,128)S(1)}, f32[2,64]{1,0:T(2,128)}, u32[]{:S(2)}) copy-start(f32[2,64]{1,0:T(2,128)} %param.14) | copy-start | bytes 1540
  0.0 24.8 %copy-start.1 = (s32[16,12]{1,0:T(8,128)S(1)}, s32[16,12]{1,0:T(8,128)}, u32[]{:S(2)}) copy-start(s32[16,12]{1,0:T(8,128)} %param.18) | copy-start | bytes 2308
  0.0 24.9 %copy-start.7 = (f32[64]{0:T(128)S(1)}, f32[64]{0:T(128)}, u32[]{:S(2)}) copy-start(f32[64]{0:T(128)} %param.11) | copy-start | bytes 772
  2.8 22.2 %collective-permute-start = (bf16[64,4,4,384]{3,0,2,1:T(8,128)(2,1)S(1)}, bf16[64,4,4,384]{3,0,2,1:T(8,128)(2,1)S(1)}, u32[]{:S(2)}, u32[]{:S(2)}) collective-permute-start(bf16[64,4,4,384]{3,0,2,1:T(8,128)(2,1)S(1)} %copy.49), channel_id=1, source_target_pairs={{0,1},{1,2},{2,3},{3,4},{4,5},{5,6},{6,7},{8,9},{9,10},{10,11},{11... | collective-permute-start | bytes 2359304 | tf_op jit(solution)/shard_map/ppermute | solution.py:15
  6.3 19.2 %collective-permute-start.1 = (bf16[64,4,4,384]{3,0,2,1:T(8,128)(2,1)S(1)}, bf16[64,4,4,384]{3,0,2,1:T(8,128)(2,1)S(1)}, u32[]{:S(2)}, u32[]{:S(2)}) collective-permute-start(bf16[64,4,4,384]{3,0,2,1:T(8,128)(2,1)S(1)} %copy.50), channel_id=1, source_target_pairs={{1,0},{2,1},{3,2},{4,3},{5,4},{6,5},{7,6},{9,8},{10,9},{11,10},{12... | collective-permute-start | bytes 2359304 | tf_op jit(solution)/shard_map/ppermute | solution.py:18
  65.5 31.8 %copy-start.8 = (bf16[2,64,64]{2,1,0:T(8,128)(2,1)S(1)}, bf16[2,64,64]{2,1,0:T(8,128)(2,1)}, u32[]{:S(2)}) copy-start(bf16[2,64,64]{2,1,0:T(8,128)(2,1)} %param.13) | copy-start | bytes 49156
  104.3 2.7 copy-start
  107.2 13.1 %collective-permute-start.2 = (bf16[64,4,4,384]{3,0,2,1:T(8,128)(2,1)S(1)}, bf16[64,4,4,384]{3,0,2,1:T(8,128)(2,1)S(1)}, u32[]{:S(2)}, u32[]{:S(2)}) collective-permute-start(bf16[64,4,4,384]{3,0,2,1:T(8,128)(2,1)S(1)} %get-tuple-element.7), channel_id=1, source_target_pairs={{0,1},{1,2},{2,3},{3,4},{4,5},{5,6},{6,7},{8,9},{9,10},{10,11},{11... | collective-permute-start | bytes 2359304 | tf_op jit(solution)/shard_map/ppermute | solution.py:15
  111.4 13.3 %collective-permute-start.3 = (bf16[64,4,4,384]{3,0,2,1:T(8,128)(2,1)S(1)}, bf16[64,4,4,384]{3,0,2,1:T(8,128)(2,1)S(1)}, u32[]{:S(2)}, u32[]{:S(2)}) collective-permute-start(bf16[64,4,4,384]{3,0,2,1:T(8,128)(2,1)S(1)} %get-tuple-element.8), channel_id=1, source_target_pairs={{1,0},{2,1},{3,2},{4,3},{5,4},{6,5},{7,6},{9,8},{10,9},{11,10},{12... | collective-permute-start | bytes 2359304 | tf_op jit(solution)/shard_map/ppermute | solution.py:18
  197.3 7.5 %copy-start.2 = (s32[8,24]{1,0:T(8,128)S(1)}, s32[8,24]{1,0:T(8,128)}, u32[]{:S(2)}) copy-start(s32[8,24]{1,0:T(8,128)} %param.19) | copy-start | bytes 2308
  197.3 7.6 %copy-start.6 = (f32[2,64]{1,0:T(2,128)S(1)}, f32[2,64]{1,0:T(2,128)}, u32[]{:S(2)}) copy-start(f32[2,64]{1,0:T(2,128)} %param.17) | copy-start | bytes 1540
  197.3 7.7 %copy-start.4 = (f32[2,2,64,5]{2,1,3,0:T(2,128)S(1)}, f32[2,2,64,5]{2,1,3,0:T(2,128)}, u32[]{:S(2)}) copy-start(f32[2,2,64,5]{2,1,3,0:T(2,128)} %param.15) | copy-start | bytes 15364
  197.3 177.4 %all-to-all-start = ((bf16[64,16,12,384]{3,0,2,1:T(8,128)(2,1)}), bf16[64,16,12,384]{3,0,2,1:T(8,128)(2,1)}, u32[]{:S(2)}, u32[]{:S(2)}) async-start(bf16[64,16,12,384]{3,0,2,1:T(8,128)(2,1)} %select_select_fusion.1), calls=%async_computation | async-start | bytes 18874368 | tf_op jit(solution)/shard_map/all_to_all | solution.py:85
  397.4 23.3 %copy-start.9 = (bf16[2,64,64]{2,1,0:T(8,128)(2,1)S(1)}, bf16[2,64,64]{2,1,0:T(8,128)(2,1)}, u32[]{:S(2)}) copy-start(bf16[2,64,64]{2,1,0:T(8,128)(2,1)} %param.16) | copy-start | bytes 49156
where the time goes:
time: 534 us; the launch traced here: 531 us
  waiting for transfers between devices  181 us (34%)
  other arithmetic  158 us (30%)
  matrix products  114 us (21%)
  local copies, waits for them, and re-layouts  47.1 us (9%)
  starting transfers between devices  19.1 us (4%)
  blocking collectives  12 us (2%)
    all_to_all x1, waiting for transfers between devices, per_device(): lax.all_to_all(picked.reshape(channels, blocks, capacity, samples), 'shot...  170 us
    dot_general x4, matrix products, mixing(): jnp.einsum('oc,cabd->oabd', weight, inputs, preferred_element_type=jnp.fl...  114 us
    add x4, other arithmetic, dilated(): summed + kernel[:, offset].reshape(target) * lax.slice_in_dim(padded, 2 *...  94.1 us
    convert_element_type x1, other arithmetic, stencil(): return zero_conv(across, kernel_pair[1], 3).astype(jnp.bfloat16)  31.8 us
    gather x1, local copies, waits for them, and re-layouts, per_device(): unpack_picked = jnp.take(flattened, jnp.maximum(keep_index, 0), axis=1)  13.8 us
    convert_element_type x1, local copies, waits for them, and re-layouts, per_device(): (mixing(mixed_in, recv_mix[depth], recv_bias[depth]) * live_mask).astype(...  13 us
    gather x1, local copies, waits for them, and re-layouts, per_device(): picked = jnp.take(flattened, jnp.maximum(send_index, 0), axis=1)  12.9 us
    psum x1, blocking collectives, per_device(): lax.psum(jnp.sum(jnp.square(shot_feats.astype(jnp.float32)), axis=(0, 2,...  12 us
  transfers between devices with their start and end apart: 5, of which 3 were waited for; matrix products, arithmetic and copies ran while one was open for 1% of the time, Pallas kernels for 0%

commit v1 on v0

v1 whole, which is shorter than its diff:
```python
import functools

import jax
import jax.numpy as jnp
from jax import lax
from jax.experimental import pallas as pl
from jax.experimental.pallas import tpu as pltpu
from jax.sharding import PartitionSpec as P

TRACES = 256
LAYERS = 2
HALO = 8
GROUP = 8
LANES = 128
BF16 = jnp.bfloat16
F32 = jnp.float32


def lagged(values, lag):
    if lag == 0:
        return values
    samples = values.shape[1]
    turned = pltpu.roll(values, (-lag) % samples, 1)
    lane = lax.broadcasted_iota(jnp.int32, values.shape, 1)
    inside = lane < samples - lag if lag > 0 else lane >= -lag
    return jnp.where(inside, turned, jnp.zeros((), values.dtype))


def group_linear(source, first, taps, weight, count):
    channels, samples = source.shape[1:]
    part = 16
    tiles = samples // LANES
    filtered = [[[None] * tiles for _ in range(channels // part)] for _ in range(count)]
    for h in range(channels // part):
        rows_at = slice(h * part, (h + 1) * part)
        for j in range(tiles):
            lanes_at = slice(j * LANES, (j + 1) * LANES)
            tap = [taps[k, rows_at, :] for k in range(5)]
            rows = [source[first + i, rows_at, lanes_at].astype(F32) for i in range(count + 8)]
            for q in range(count):
                term = [rows[q + 2 * k] * tap[k] for k in range(5)]
                total = ((term[0] + term[1]) + (term[2] + term[3])) + term[4]
                filtered[q][h][j] = total.astype(BF16)
    outs = []
    for q in range(count):
        across = jnp.concatenate(
            [jnp.concatenate(pieces, axis=1) for pieces in filtered[q]], axis=0
        )
        stacked = jnp.concatenate([lagged(across, 2 * k - 4) for k in range(5)], axis=0)
        outs.append(jnp.dot(weight[...], stacked, preferred_element_type=F32))
    return outs


def shot_kernel(
    inverse_rms,
    slot_of,
    edges,
    main,
    low,
    high,
    taps,
    weights,
    bias,
    packed,
    turned,
    grid_in,
    first_out,
    last_out,
    sems,
):
    shot = pl.program_id(0)
    shots = pl.num_programs(0)
    channels, _, here, samples = main.shape
    span = here + 2 * HALO
    tiles = samples // LANES

    def load_channel(i, _):
        for q in range(2):
            c = i * 2 + q
            base = pl.multiple_of(c * span, 8)
            for j in range(tiles):
                at = slice(j * LANES, (j + 1) * LANES)
                turned[j, pl.ds(base, HALO), :] = low[c, 0, :, at].astype(F32)
                turned[j, pl.ds(base + HALO, here), :] = main[c, 0, :, at].astype(F32)
                turned[j, pl.ds(base + HALO + here, HALO), :] = high[c, 0, :, at].astype(F32)
        return 0

    lax.fori_loop(0, channels // 2, load_channel, 0)

    def gather_trace(i, _):
        for q in range(4):
            t = i * 4 + q
            for j in range(tiles):
                at = slice(j * LANES, (j + 1) * LANES)
                grid_in[t, :, at] = turned[j, pl.ds(t, channels, stride=span), :].astype(BF16)
        return 0

    lax.fori_loop(0, span // 4, gather_trace, 0)

    scale = inverse_rms[shot]
    count = here + 8

    def first_layer(i, _):
        outs = group_linear(grid_in, i * GROUP, taps.at[0], weights.at[0], GROUP)
        for q in range(GROUP):
            t = i * GROUP + q
            value = jnp.maximum(outs[q] * scale + bias[0], 0.0)
            first_out[t] = value.astype(BF16)
        return 0

    lax.fori_loop(0, count // GROUP, first_layer, 0)

    @pl.when(edges[0] == 1)
    def _():
        first_out[0:4] = jnp.zeros((4, channels, samples), BF16)

    @pl.when(edges[1] == 1)
    def _():
        first_out[here + 4 : here + 8] = jnp.zeros((4, channels, samples), BF16)

    half = lax.rem(shot, 2)

    def drain(which):
        pltpu.make_async_copy(
            last_out.at[which], packed.at[pl.ds(0, here)], sems.at[which]
        ).wait()

    @pl.when(shot >= 2)
    def _():
        drain(half)

    def second_layer(i, _):
        outs = group_linear(first_out, i * GROUP, taps.at[1], weights.at[1], GROUP)
        for q in range(GROUP):
            t = i * GROUP + q
            value = jnp.maximum(outs[q] + bias[1], 0.0)
            last_out[half, t] = value.astype(BF16)
        for q in range(GROUP):
            t = i * GROUP + q
            pltpu.make_async_copy(
                last_out.at[half, t], packed.at[slot_of[shot * here + t]], sems.at[half]
            ).start()
        return 0

    lax.fori_loop(0, here // GROUP, second_layer, 0)

    @pl.when(shot == shots - 1)
    def _():
        drain(1 - half)
        drain(half)


def recv_kernel(
    keep,
    live_count,
    buffer,
    taps,
    weights,
    bias,
    out,
    gathered,
    middle,
    turned,
    sems,
):
    row = pl.program_id(0)
    rows = pl.num_programs(0)
    channels, _, fold, samples = out.shape
    tiles = samples // LANES
    half = lax.rem(row, 2)

    def fetch(r, into):
        def one(k, _):
            pltpu.make_async_copy(
                buffer.at[keep[r * fold + k]], gathered.at[into, 4 + k], sems.at[into]
            ).start()
            return 0

        lax.fori_loop(0, fold, one, 0)

    @pl.when(row == 0)
    def _():
        fetch(0, 0)
        edge = jnp.zeros((4, channels, samples), BF16)
        for which in range(2):
            gathered[which, 0:4] = edge
            gathered[which, fold + 4 : fold + 8] = edge
        middle[0:4] = edge
        middle[fold + 4 : fold + 8] = edge

    @pl.when(row + 1 < rows)
    def _():
        fetch(row + 1, 1 - half)

    pltpu.make_async_copy(
        buffer.at[pl.ds(0, fold)], gathered.at[half, pl.ds(4, fold)], sems.at[half]
    ).wait()
    live = live_count[row]

    def clear(k, _):
        gathered[half, 4 + k] = jnp.zeros((channels, samples), BF16)
        return 0

    lax.fori_loop(live, fold, clear, 0)
    groups = (live + GROUP - 1) // GROUP

    def first_layer(i, _):
        outs = group_linear(gathered.at[half], i * GROUP, taps.at[0], weights.at[0], GROUP)
        for q in range(GROUP):
            k = i * GROUP + q
            value = jnp.maximum(outs[q] + bias[0], 0.0)
            middle[4 + k] = jnp.where(k < live, value, 0.0).astype(BF16)
        return 0

    lax.fori_loop(0, groups, first_layer, 0)

    def clear_rest(k, _):
        middle[4 + k] = jnp.zeros((channels, samples), BF16)
        for j in range(tiles):
            turned[j, pl.ds(k, channels, stride=fold), :] = jnp.zeros((channels, LANES), F32)
        return 0

    lax.fori_loop(groups * GROUP, fold, clear_rest, 0)

    def second_layer(i, _):
        outs = group_linear(middle, i * GROUP, taps.at[1], weights.at[1], GROUP)
        for q in range(GROUP):
            k = i * GROUP + q
            value = jnp.where(k < live, jnp.maximum(outs[q] + bias[1], 0.0), 0.0)
            for j in range(tiles):
                turned[j, pl.ds(k, channels, stride=fold), :] = value[:, j * LANES : (j + 1) * LANES]
        return 0

    lax.fori_loop(0, groups, second_layer, 0)

    def store_channel(i, _):
        for q in range(4):
            c = i * 4 + q
            base = pl.multiple_of(c * fold, 8)
            for j in range(tiles):
                out[c, 0, :, j * LANES : (j + 1) * LANES] = turned[j, pl.ds(base, fold), :].astype(BF16)
        return 0

    lax.fori_loop(0, channels // 4, store_channel, 0)


def whole(*shape):
    return pl.BlockSpec(shape, lambda *_: (0,) * len(shape))


def tap_tables(taps):
    table = jnp.swapaxes(taps[:, 0], 1, 2)[..., None]
    return jnp.broadcast_to(table, table.shape[:-1] + (LANES,)).astype(F32)


def mix_tables(mix, taps, gain):
    layers, outs, channels = mix.shape
    product = mix.astype(F32)[:, :, None, :] * jnp.swapaxes(taps[:, 1], 1, 2)[:, None, :, :]
    if gain is not None:
        product = product * gain
    return product.reshape(layers, outs, 5 * channels).astype(BF16)


def per_device(
    shot_feats,
    norm_gain,
    shot_taps,
    shot_mix,
    shot_bias,
    recv_taps,
    recv_mix,
    recv_bias,
    pack_index,
    recv_index,
):
    channels, shots_here, here, samples = shot_feats.shape
    blocks, capacity = pack_index.shape
    rows_here, fold = recv_index.shape
    slots = blocks * capacity
    span = here + 2 * HALO

    tiles_all = lax.axis_size("recv")
    tile = lax.axis_index("recv")
    forward = [(i, i + 1) for i in range(tiles_all - 1)]
    backward = [(i + 1, i) for i in range(tiles_all - 1)]
    low = lax.ppermute(shot_feats[:, :, here - HALO :, :], "recv", forward)
    high = lax.ppermute(shot_feats[:, :, :HALO, :], "recv", backward)
    energy = lax.psum(jnp.sum(jnp.square(shot_feats.astype(F32)), axis=(0, 2, 3)), "recv")
    inverse_rms = 1.0 / jnp.sqrt(energy / (channels * TRACES * samples) + 1e-05)

    packs = pack_index.reshape(-1)
    trace_id = jnp.arange(shots_here * here, dtype=jnp.int32)
    slot_id = jnp.arange(slots, dtype=jnp.int32)
    slot_of = jnp.sum(
        jnp.where(packs[None, :] == trace_id[:, None], slot_id[None, :], 0), axis=1
    ).astype(jnp.int32)
    edges = jnp.stack([tile == 0, tile == tiles_all - 1]).astype(jnp.int32)

    gain_rows = jnp.stack([norm_gain] + [jnp.ones_like(norm_gain)] * (LAYERS - 1))
    weights = mix_tables(shot_mix, shot_taps, gain_rows[:, None, None, :])
    bias = jnp.broadcast_to(shot_bias[:, :, None], shot_bias.shape + (samples,))
    smem = pl.BlockSpec(memory_space=pltpu.SMEM)
    packed = pl.pallas_call(
        shot_kernel,
        grid=(shots_here,),
        in_specs=[
            smem,
            smem,
            smem,
            pl.BlockSpec((channels, 1, here, samples), lambda s: (0, s, 0, 0)),
            pl.BlockSpec((channels, 1, HALO, samples), lambda s: (0, s, 0, 0)),
            pl.BlockSpec((channels, 1, HALO, samples), lambda s: (0, s, 0, 0)),
            whole(LAYERS, 5, channels, LANES),
            whole(LAYERS, channels, 5 * channels),
            whole(LAYERS, channels, samples),
        ],
        out_specs=pl.BlockSpec(memory_space=pl.ANY),
        out_shape=jax.ShapeDtypeStruct((slots, channels, samples), BF16),
        scratch_shapes=[
            pltpu.VMEM((samples // LANES, channels * span, LANES), F32),
            pltpu.VMEM((span, channels, samples), BF16),
            pltpu.VMEM((here + 8, channels, samples), BF16),
            pltpu.VMEM((2, here, channels, samples), BF16),
            pltpu.SemaphoreType.DMA((2,)),
        ],
        compiler_params=pltpu.CompilerParams(vmem_limit_bytes=48 * 2**20),
        name="shot_domain",
    )(inverse_rms, slot_of, edges, shot_feats, low, high, tap_tables(shot_taps), weights, bias)

    buffer = lax.all_to_all(
        packed.reshape(blocks, capacity, channels, samples),
        "shot",
        split_axis=0,
        concat_axis=0,
        tiled=True,
    ).reshape(slots, channels, samples)

    keep = jnp.maximum(recv_index.reshape(-1), 0)
    live_count = jnp.sum(recv_index >= 0, axis=1).astype(jnp.int32)
    recv_bias_rows = jnp.broadcast_to(recv_bias[:, :, None], recv_bias.shape + (samples,))
    return pl.pallas_call(
        recv_kernel,
        grid=(rows_here,),
        in_specs=[
            smem,
            smem,
            pl.BlockSpec(memory_space=pl.ANY),
            whole(LAYERS, 5, channels, LANES),
            whole(LAYERS, channels, 5 * channels),
            whole(LAYERS, channels, samples),
        ],
        out_specs=pl.BlockSpec((channels, 1, fold, samples), lambda r: (0, r, 0, 0)),
        out_shape=jax.ShapeDtypeStruct((channels, rows_here, fold, samples), BF16),
        scratch_shapes=[
            pltpu.VMEM((2, fold + 8, channels, samples), BF16),
            pltpu.VMEM((fold + 8, channels, samples), BF16),
            pltpu.VMEM((samples // LANES, channels * fold, LANES), F32),
            pltpu.SemaphoreType.DMA((2,)),
        ],
        compiler_params=pltpu.CompilerParams(vmem_limit_bytes=48 * 2**20),
        name="recv_domain",
    )(
        keep,
        live_count,
        buffer,
        tap_tables(recv_taps),
        mix_tables(recv_mix, recv_taps, None),
        recv_bias_rows,
    )


def solution(mesh):
    return jax.shard_map(
        per_device,
        mesh=mesh,
        in_specs=(
            P(None, "shot", "recv", None),
            P(),
            P(),
            P(),
            P(),
            P(),
            P(),
            P(),
            P(("shot", "recv"), None),
            P(("shot", "recv"), None),
        ),
        out_specs=P(None, ("shot", "recv"), None, None),
        check_vma=False,
    )
```

time: 534 us -> 293 us (0.55)
  the two profiles are of different devices: /device:TPU:85 before, /device:TPU:114 now
where the time goes in v1:
time: 293 us
  waiting for transfers between devices  164 us (56%)
  Pallas kernels  79.5 us (27%)
  blocking collectives  24.5 us (8%)
  starting transfers between devices  12.6 us (4%)
  local copies, waits for them, and re-layouts  7.52 us (3%)
  other arithmetic  3.73 us (1%)
    all_to_all x1, waiting for transfers between devices, per_device(): lax.all_to_all(packed.reshape(blocks, capacity, channels, samples), 'shot...  164 us
    pallas_call x1, Pallas kernels, per_device(): pl.pallas_call(shot_kernel, grid=(shots_here,), in_specs=[smem, smem, sme...  41.7 us
    pallas_call x1, Pallas kernels, per_device(): pl.pallas_call(recv_kernel, grid=(rows_here,), in_specs=[smem, smem, pl.B...  37.8 us
    psum x1, blocking collectives, per_device(): lax.psum(jnp.sum(jnp.square(shot_feats.astype(F32)), axis=(0, 2, 3)), 're...  24.5 us
    all_to_all x1, starting transfers between devices, per_device(): lax.all_to_all(packed.reshape(blocks, capacity, channels, samples), 'shot...  7.08 us
  transfers between devices with their start and end apart: 3, of which 1 were waited for; matrix products, arithmetic and copies ran while one was open for 2% of the time, Pallas kernels for 0%

profile of v1, /device:TPU:114, one launch (start us, length us, event | category | flops | bytes accessed | tf_op | source)
XLA Modules:
  0.0 292.6 jit_solution(17767571515320105551)
XLA Ops:
  0.0 0.0 copy-start
  0.0 0.0 copy-start.3
  0.0 0.0 copy-start.1
  0.0 0.0 copy-start.6
  0.0 4.1 %fusion = (bf16[64,4,8,384]{3,2,1,0:T(8,128)(2,1)}, bf16[64,4,8,384]{3,2,1,0:T(8,128)(2,1)}) fusion(bf16[64,4,32,384]{3,2,1,0:T(8,128)(2,1)} %main.1), kind=kLoop, calls=%fused_computation.13 | loop fusion | bytes 6291456 | tf_op jit(solution)/shard_map/slice | solution.py:287
  4.1 1.9 collective-permute-start
  6.0 3.6 %collective-permute-start.1 = (bf16[64,4,8,384]{3,2,1,0:T(8,128)(2,1)}, bf16[64,4,8,384]{3,2,1,0:T(8,128)(2,1)S(1)}, u32[]{:S(2)}, u32[]{:S(2)}) collective-permute-start(bf16[64,4,8,384]{3,2,1,0:T(8,128)(2,1)} %get-tuple-element.5), channel_id=1, source_target_pairs={{1,0},{2,1},{3,2},{4,3},{5,4},{6,5},{7,6},{9,8},{10,9},{11,10},{12... | collective-permute-start | bytes 4718600 | tf_op jit(solution)/shard_map/ppermute | solution.py:287
  9.6 0.0 copy-done
  9.6 1.8 multiply_reduce_fusion
  11.4 24.5 %psum.7 = f32[4]{0:T(128)} all-reduce(f32[4]{0:T(128)S(1)} %multiply_reduce_fusion), channel_id=1, replica_groups=mesh['shot'=16,'recv'=8] {'recv'}, use_global_device_ids=true, to_apply=%region_2.3 | all-reduce | flops 4 | bytes 32 | tf_op jit(solution)/shard_map/psum | solution.py:288
  35.9 0.0 copy-done.3
  36.0 0.1 mul.51
  36.0 0.0 copy-done.1
  36.0 0.1 copy.25
  36.2 0.8 copy.28
  37.0 0.7 stack.19
  37.7 0.1 mul.55
  37.8 0.8 eq.21
  38.5 0.1 add_convert_fusion.edges
  38.6 0.1 select_reduce_fusion.slot_of
  38.7 0.7 add_rsqrt_fusion.inverse_rms
  39.4 1.0 multiply_convert_fusion.1.weights
  40.3 0.0 collective-permute-done.low
  40.4 0.0 collective-permute-done.1.high
  40.4 0.1 broadcast_in_dim.22.taps
  40.5 0.0 copy-done.6
  40.5 0.1 broadcast_in_dim.23.bias
  40.6 41.7 %shot_domain.1 = bf16[192,64,384]{2,1,0:T(8,128)(2,1)} custom-call(f32[4]{0:T(128)S(1)} %add_rsqrt_fusion.inverse_rms, s32[128]{0:T(128)S(1)} %select_reduce_fusion.slot_of, s32[2]{0:T(128)S(1)} %add_convert_fusion.edges, bf16[64,4,32,384]{3,2,1,0:T(8,128)(2,1)} %main.1, bf16[64,4,8,384]{3,2,1,0:T(8,128)(2,1)S(1)} %collective-permute-done.low, ...), custom_call_target="tpu_custom_call" | custom-call | tf_op jit(solution)/shard_map/shot_domain/pallas_call | solution.py:303
  82.3 0.0 copy-start.4
  82.3 0.0 copy-start.2
  82.3 0.0 copy-start.5
  82.3 0.0 copy-start.7
  82.3 7.1 %all-to-all-start = ((bf16[16,12,64,384]{3,2,1,0:T(8,128)(2,1)}), bf16[16,12,64,384]{3,2,1,0:T(8,128)(2,1)}, u32[]{:S(2)}, u32[]{:S(2)}) async-start(bf16[16,12,64,384]{3,2,1,0:T(8,128)(2,1)} %bitcast.23), calls=%async_computation | async-start | bytes 18874368 | tf_op jit(solution)/shard_map/all_to_all | solution.py:330
  89.4 0.0 copy-done.4
  89.5 0.1 mul.60
  89.5 0.0 copy-done.2
  89.5 0.1 copy.31
  89.7 0.1 copy.34
  89.8 0.0 copy-done.5
  89.8 0.1 convert_reduce_fusion
  89.9 0.1 max.10.keep
  90.1 164.5 %all-to-all-done = bf16[16,12,64,384]{3,2,1,0:T(8,128)(2,1)} async-done(((bf16[16,12,64,384]{3,2,1,0:T(8,128)(2,1)}), bf16[16,12,64,384]{3,2,1,0:T(8,128)(2,1)}, u32[]{:S(2)}, u32[]{:S(2)}) %all-to-all-start) | async-done | bytes 9437216 | tf_op jit(solution)/shard_map/all_to_all | solution.py:330
  254.5 0.1 broadcast_in_dim.24.taps
  254.7 0.0 copy-done.7
  254.7 0.1 broadcast_in_dim.25.bias
  254.8 37.8 %recv_domain.1 = bf16[64,8,24,384]{3,2,1,0:T(8,128)(2,1)} custom-call(s32[192]{0:T(256)S(1)} %max.10.keep, s32[8]{0:T(128)S(1)} %get-tuple-element.11.live_count, bf16[192,64,384]{2,1,0:T(8,128)(2,1)} %bitcast.9.buffer, f32[2,5,64,128]{3,2,1,0:T(8,128)S(1)} %broadcast_in_dim.24.taps, bf16[2,64,320]{2,1,0:T(8,128)(2,1)S(1)} %multiply_convert_fusion.weights, ...), custom_call_target="tpu_custom_call" | custom-call | tf_op jit(solution)/shard_map/recv_domain/pallas_call | solution.py:341
  (12 shorter events, 0.1 us)
Async XLA Ops:
  0.0 9.6 %copy-start = (bf16[64,4,32,384]{3,2,1,0:T(8,128)(2,1)S(1)}, bf16[64,4,32,384]{3,2,1,0:T(8,128)(2,1)}, u32[]{:S(2)}) copy-start(bf16[64,4,32,384]{3,2,1,0:T(8,128)(2,1)} %main.1) | copy-start | bytes 18874372
  0.0 35.9 %copy-start.3 = (f32[2,2,64,5]{2,1,3,0:T(2,128)S(1)}, f32[2,2,64,5]{2,1,3,0:T(2,128)}, u32[]{:S(2)}) copy-start(f32[2,2,64,5]{2,1,3,0:T(2,128)} %param.12) | copy-start | bytes 15364
  0.0 36.0 %copy-start.1 = (bf16[2,64,64]{2,1,0:T(8,128)(2,1)S(1)}, bf16[2,64,64]{2,1,0:T(8,128)(2,1)}, u32[]{:S(2)}) copy-start(bf16[2,64,64]{2,1,0:T(8,128)(2,1)} %param.13) | copy-start | bytes 49156
  0.0 40.5 %copy-start.6 = (f32[2,64]{1,0:T(2,128)S(1)}, f32[2,64]{1,0:T(2,128)}, u32[]{:S(2)}) copy-start(f32[2,64]{1,0:T(2,128)} %param.14) | copy-start | bytes 1540
  4.1 36.3 %collective-permute-start = (bf16[64,4,8,384]{3,2,1,0:T(8,128)(2,1)}, bf16[64,4,8,384]{3,2,1,0:T(8,128)(2,1)S(1)}, u32[]{:S(2)}, u32[]{:S(2)}) collective-permute-start(bf16[64,4,8,384]{3,2,1,0:T(8,128)(2,1)} %get-tuple-element.6), channel_id=1, source_target_pairs={{0,1},{1,2},{2,3},{3,4},{4,5},{5,6},{6,7},{8,9},{9,10},{10,11},{11... | collective-permute-start | bytes 4718600 | tf_op jit(solution)/shard_map/ppermute | solution.py:286
  6.0 34.4 %collective-permute-start.1 = (bf16[64,4,8,384]{3,2,1,0:T(8,128)(2,1)}, bf16[64,4,8,384]{3,2,1,0:T(8,128)(2,1)S(1)}, u32[]{:S(2)}, u32[]{:S(2)}) collective-permute-start(bf16[64,4,8,384]{3,2,1,0:T(8,128)(2,1)} %get-tuple-element.5), channel_id=1, source_target_pairs={{1,0},{2,1},{3,2},{4,3},{5,4},{6,5},{7,6},{9,8},{10,9},{11,10},{12... | collective-permute-start | bytes 4718600 | tf_op jit(solution)/shard_map/ppermute | solution.py:287
  82.3 7.1 %copy-start.4 = (f32[2,2,64,5]{2,1,3,0:T(2,128)S(1)}, f32[2,2,64,5]{2,1,3,0:T(2,128)}, u32[]{:S(2)}) copy-start(f32[2,2,64,5]{2,1,3,0:T(2,128)} %param.15) | copy-start | bytes 15364
  82.3 7.2 %copy-start.2 = (bf16[2,64,64]{2,1,0:T(8,128)(2,1)S(1)}, bf16[2,64,64]{2,1,0:T(8,128)(2,1)}, u32[]{:S(2)}) copy-start(bf16[2,64,64]{2,1,0:T(8,128)(2,1)} %param.16) | copy-start | bytes 49156
  82.3 7.5 %copy-start.5 = (s32[8,24]{1,0:T(8,128)S(1)}, s32[8,24]{1,0:T(8,128)}, u32[]{:S(2)}) copy-start(s32[8,24]{1,0:T(8,128)} %param.19) | copy-start | bytes 2308
  82.3 172.4 %copy-start.7 = (f32[2,64]{1,0:T(2,128)S(1)}, f32[2,64]{1,0:T(2,128)}, u32[]{:S(2)}) copy-start(f32[2,64]{1,0:T(2,128)} %param.17) | copy-start | bytes 1540
  82.3 172.2 %all-to-all-start = ((bf16[16,12,64,384]{3,2,1,0:T(8,128)(2,1)}), bf16[16,12,64,384]{3,2,1,0:T(8,128)(2,1)}, u32[]{:S(2)}, u32[]{:S(2)}) async-start(bf16[16,12,64,384]{3,2,1,0:T(8,128)(2,1)} %bitcast.23), calls=%async_computation | async-start | bytes 18874368 | tf_op jit(solution)/shard_map/all_to_all | solution.py:330

commit v2 on v1

v2 whole, which is shorter than its diff:
```python
import jax
import jax.numpy as jnp
from jax import lax
from jax.experimental import pallas as pl
from jax.experimental.pallas import tpu as pltpu
from jax.sharding import PartitionSpec as P

TRACES = 256
LAYERS = 2
HALO = 8
GROUP = 8
CHUNKS = 3
PITCH = 33
FOLDP = 25
LANES = 128
BF16 = jnp.bfloat16
F32 = jnp.float32


def lagged(values, lag):
    if lag == 0:
        return values
    samples = values.shape[1]
    turned = pltpu.roll(values, (-lag) % samples, 1)
    lane = lax.broadcasted_iota(jnp.int32, values.shape, 1)
    inside = lane < samples - lag if lag > 0 else lane >= -lag
    return jnp.where(inside, turned, jnp.zeros((), values.dtype))


def group_linear(source, first, taps, weight, count):
    split = len(source.shape) == 4
    channels = source.shape[-2]
    part = 16
    tiles = source.shape[0] if split else source.shape[2] // LANES
    filtered = [[[None] * tiles for _ in range(channels // part)] for _ in range(count)]
    for h in range(channels // part):
        rows_at = slice(h * part, (h + 1) * part)
        for j in range(tiles):
            lanes_at = slice(j * LANES, (j + 1) * LANES)
            tap = [taps[k, rows_at, :] for k in range(5)]
            rows = [
                (
                    source[j, first + i, rows_at, :]
                    if split
                    else source[first + i, rows_at, lanes_at]
                ).astype(F32)
                for i in range(count + 8)
            ]
            for q in range(count):
                term = [rows[q + 2 * k] * tap[k] for k in range(5)]
                total = ((term[0] + term[1]) + (term[2] + term[3])) + term[4]
                filtered[q][h][j] = total.astype(BF16)
    outs = []
    for q in range(count):
        across = jnp.concatenate(
            [jnp.concatenate(pieces, axis=1) for pieces in filtered[q]], axis=0
        )
        stacked = jnp.concatenate([lagged(across, 2 * k - 4) for k in range(5)], axis=0)
        outs.append(jnp.dot(weight[...], stacked, preferred_element_type=F32))
    return outs


def last_layer(source, first, trace, base, send, packed, tables, staged, half, sems, at):
    taps, weights, bias = tables
    outs = group_linear(source, first, taps.at[1], weights.at[1], GROUP)
    for q in range(GROUP):
        value = jnp.maximum(outs[q] + bias[1], 0.0).astype(BF16)
        for j in range(CHUNKS):
            staged[half, j, at + q] = value[:, j * LANES : (j + 1) * LANES]
    for q in range(GROUP):
        slot = send[base + trace + q]
        for j in range(CHUNKS):
            pltpu.make_async_copy(
                staged.at[half, j, at + q], packed[j].at[slot], sems.at[half]
            ).start()


def drain(staged, packed, sems, half):
    for j in range(CHUNKS):
        pltpu.make_async_copy(
            staged.at[half, j], packed[j].at[pl.ds(0, staged.shape[2])], sems.at[half]
        ).wait()


def regroup(turned, grid_in, channels):
    span = grid_in.shape[0]

    def gather_trace(i, _):
        for q in range(8):
            t = i * 8 + q
            for j in range(turned.shape[0]):
                at = slice(j * LANES, (j + 1) * LANES)
                grid_in[t, :, at] = turned[j, pl.ds(t, channels, stride=PITCH), :].astype(BF16)
        return 0

    lax.fori_loop(0, span // 8, gather_trace, 0)


def inner_kernel(inverse_rms, send, main, taps, weights, bias, middle, *rest):
    packed, (turned, grid_in, staged, sems) = rest[:CHUNKS], rest[CHUNKS:]
    shot = pl.program_id(0)
    channels, _, here, samples = main.shape
    half = lax.rem(shot, 2)

    def load_channel(i, _):
        for q in range(4):
            c = i * 4 + q
            base = c * PITCH
            for j in range(turned.shape[0]):
                at = slice(j * LANES, (j + 1) * LANES)
                turned[j, pl.ds(base, here), :] = main[c, 0, :, at].astype(F32)
        return 0

    lax.fori_loop(0, channels // 4, load_channel, 0)
    regroup(turned, grid_in, channels)
    scale = inverse_rms[shot]

    def first_layer(i, _):
        outs = group_linear(grid_in, i * GROUP, taps.at[0], weights.at[0], GROUP)
        for q in range(GROUP):
            value = jnp.maximum(outs[q] * scale + bias[0], 0.0)
            middle[0, i * GROUP + q] = value.astype(BF16)
        return 0

    lax.fori_loop(0, (here - 8) // GROUP, first_layer, 0)

    @pl.when(shot >= 2)
    def _():
        drain(staged, packed, sems, half)

    def second_layer(i, _):
        last_layer(
            middle.at[0],
            i * GROUP,
            8 + i * GROUP,
            shot * here,
            send,
            packed,
            (taps, weights, bias),
            staged,
            half,
            sems,
            i * GROUP,
        )
        return 0

    lax.fori_loop(0, (here - 16) // GROUP, second_layer, 0)

    @pl.when(shot == pl.num_programs(0) - 1)
    def _():
        drain(staged, packed, sems, 1 - half)
        drain(staged, packed, sems, half)


def edge_kernel(inverse_rms, send, edges, main, low, high, middle, taps, weights, bias, *rest):
    rest = rest[CHUNKS:]
    packed, (turned, grid_in, joined, staged, sems) = rest[:CHUNKS], rest[CHUNKS:]
    shot = pl.program_id(0)
    channels, _, here, samples = main.shape
    span = 4 * HALO
    half = lax.rem(shot, 2)

    def load_channel(i, _):
        for q in range(4):
            c = i * 4 + q
            base = c * PITCH
            for j in range(turned.shape[0]):
                at = slice(j * LANES, (j + 1) * LANES)
                turned[j, pl.ds(base, HALO), :] = low[c, 0, :, at].astype(F32)
                turned[j, pl.ds(base + HALO, HALO), :] = main[c, 0, 0:16, at].astype(F32)[:HALO]
                turned[j, pl.ds(base + 2 * HALO, HALO), :] = main[
                    c, 0, here - 16 : here, at
                ].astype(F32)[16 - HALO :]
                turned[j, pl.ds(base + 3 * HALO, HALO), :] = high[c, 0, :, at].astype(F32)
        return 0

    lax.fori_loop(0, channels // 4, load_channel, 0)
    regroup(turned, grid_in, channels)
    scale = inverse_rms[shot]

    @pl.when(shot >= 2)
    def _():
        drain(staged, packed, sems, half)

    def one_side(side, _):
        outs = group_linear(grid_in, side * 16, taps.at[0], weights.at[0], GROUP)
        for q in range(GROUP):
            value = jnp.maximum(outs[q] * scale + bias[0], 0.0)
            joined[side, side * 8 + q] = value.astype(BF16)
            joined[side, 8 - side * 8 + q] = middle[0, side * 16 + q]

        @pl.when(edges[side] == 1)
        def _():
            joined[side, pl.ds(side * 12, 4)] = jnp.zeros((4, channels, samples), BF16)

        last_layer(
            joined.at[side],
            0,
            side * (here - 8),
            shot * here,
            send,
            packed,
            (taps, weights, bias),
            staged,
            half,
            sems,
            side * GROUP,
        )
        return 0

    lax.fori_loop(0, 2, one_side, 0)

    @pl.when(shot == pl.num_programs(0) - 1)
    def _():
        drain(staged, packed, sems, 1 - half)
        drain(staged, packed, sems, half)


def recv_kernel(
    keep,
    live_count,
    taps,
    weights,
    bias,
    *rest,
):
    buffers, (out, gathered, middle, turned, sems) = rest[:CHUNKS], rest[CHUNKS:]
    row = pl.program_id(0)
    rows = pl.num_programs(0)
    channels, _, fold, samples = out.shape
    tiles = samples // LANES
    half = lax.rem(row, 2)

    def fetch(r, into):
        def one(i, _):
            for q in range(4):
                k = i * 4 + q
                slot = keep[r * fold + k]
                for j in range(CHUNKS):
                    pltpu.make_async_copy(
                        buffers[j].at[slot], gathered.at[into, j, 4 + k], sems.at[into]
                    ).start()
            return 0

        lax.fori_loop(0, fold // 4, one, 0)

    @pl.when(row == 0)
    def _():
        fetch(0, 0)
        edge = jnp.zeros((4, channels, samples), BF16)
        for which in range(2):
            for j in range(CHUNKS):
                gathered[which, j, 0:4] = edge[:, :, :LANES]
                gathered[which, j, fold + 4 : fold + 8] = edge[:, :, :LANES]
        middle[0:4] = edge
        middle[fold + 4 : fold + 8] = edge

    @pl.when(row + 1 < rows)
    def _():
        fetch(row + 1, 1 - half)

    for j in range(CHUNKS):
        pltpu.make_async_copy(
            buffers[j].at[pl.ds(0, fold)], gathered.at[half, j, pl.ds(4, fold)], sems.at[half]
        ).wait()
    live = live_count[row]

    def clear(k, _):
        for j in range(CHUNKS):
            gathered[half, j, 4 + k] = jnp.zeros((channels, LANES), BF16)
        return 0

    lax.fori_loop(live, fold, clear, 0)
    groups = (live + GROUP - 1) // GROUP

    def first_layer(i, _):
        outs = group_linear(gathered.at[half], i * GROUP, taps.at[0], weights.at[0], GROUP)
        for q in range(GROUP):
            k = i * GROUP + q
            value = jnp.maximum(outs[q] + bias[0], 0.0)
            middle[4 + k] = jnp.where(k < live, value, 0.0).astype(BF16)
        return 0

    lax.fori_loop(0, groups, first_layer, 0)

    def clear_rest(k, _):
        middle[4 + k] = jnp.zeros((channels, samples), BF16)
        for j in range(tiles):
            turned[j, pl.ds(k, channels, stride=FOLDP), :] = jnp.zeros((channels, LANES), F32)
        return 0

    lax.fori_loop(groups * GROUP, fold, clear_rest, 0)

    def second_layer(i, _):
        outs = group_linear(middle, i * GROUP, taps.at[1], weights.at[1], GROUP)
        for q in range(GROUP):
            k = i * GROUP + q
            value = jnp.where(k < live, jnp.maximum(outs[q] + bias[1], 0.0), 0.0)
            for j in range(tiles):
                turned[j, pl.ds(k, channels, stride=FOLDP), :] = value[:, j * LANES : (j + 1) * LANES]
        return 0

    lax.fori_loop(0, groups, second_layer, 0)

    def store_channel(i, _):
        for q in range(4):
            c = i * 4 + q
            base = c * FOLDP
            for j in range(tiles):
                out[c, 0, :, j * LANES : (j + 1) * LANES] = turned[j, pl.ds(base, fold), :].astype(BF16)
        return 0

    lax.fori_loop(0, channels // 4, store_channel, 0)


def whole(*shape):
    return pl.BlockSpec(shape, lambda *_: (0,) * len(shape))


def tap_tables(taps):
    table = jnp.swapaxes(taps[:, 0], 1, 2)[..., None]
    return jnp.broadcast_to(table, table.shape[:-1] + (LANES,)).astype(F32)


def mix_tables(mix, taps, gain):
    layers, outs, channels = mix.shape
    product = mix.astype(F32)[:, :, None, :] * jnp.swapaxes(taps[:, 1], 1, 2)[:, None, :, :]
    if gain is not None:
        product = product * gain
    return product.reshape(layers, outs, 5 * channels).astype(BF16)


def per_device(
    shot_feats,
    norm_gain,
    shot_taps,
    shot_mix,
    shot_bias,
    recv_taps,
    recv_mix,
    recv_bias,
    pack_index,
    recv_index,
):
    channels, shots_here, here, samples = shot_feats.shape
    blocks, capacity = pack_index.shape
    rows_here, fold = recv_index.shape
    slots = blocks * capacity

    tiles_all = lax.axis_size("recv")
    tile = lax.axis_index("recv")
    forward = [(i, i + 1) for i in range(tiles_all - 1)]
    backward = [(i + 1, i) for i in range(tiles_all - 1)]
    energy = lax.psum(jnp.sum(jnp.square(shot_feats.astype(F32)), axis=(0, 2, 3)), "recv")
    energy, upper, lower = lax.optimization_barrier(
        (energy, shot_feats[:, :, here - HALO :, :], shot_feats[:, :, :HALO, :])
    )
    low = lax.ppermute(upper, "recv", forward)
    high = lax.ppermute(lower, "recv", backward)
    inverse_rms = 1.0 / jnp.sqrt(energy / (channels * TRACES * samples) + 1e-05)

    packs = pack_index.reshape(-1)
    trace_id = jnp.arange(shots_here * here, dtype=jnp.int32)
    slot_id = jnp.arange(slots, dtype=jnp.int32)
    slot_of = jnp.sum(
        jnp.where(packs[None, :] == trace_id[:, None], slot_id[None, :], 0), axis=1
    ).astype(jnp.int32)

    send = slot_of
    edges = jnp.stack([tile == 0, tile == tiles_all - 1]).astype(jnp.int32)

    gain_rows = jnp.stack([norm_gain] + [jnp.ones_like(norm_gain)] * (LAYERS - 1))
    weights = mix_tables(shot_mix, shot_taps, gain_rows[:, None, None, :])
    bias = jnp.broadcast_to(shot_bias[:, :, None], shot_bias.shape + (samples,))
    taps = tap_tables(shot_taps)
    smem = pl.BlockSpec(memory_space=pltpu.SMEM)
    anywhere = pl.BlockSpec(memory_space=pl.ANY)
    packed_type = jax.ShapeDtypeStruct((slots, channels, LANES), BF16)
    table_specs = [
        whole(LAYERS, 5, channels, LANES),
        whole(LAYERS, channels, 5 * channels),
        whole(LAYERS, channels, samples),
    ]
    params = pltpu.CompilerParams(vmem_limit_bytes=48 * 2**20)
    tiles = samples // LANES
    inner_rows = here - 8
    main_spec = pl.BlockSpec((channels, 1, here, samples), lambda s: (0, s, 0, 0))
    halo_spec = pl.BlockSpec((channels, 1, HALO, samples), lambda s: (0, s, 0, 0))
    middle_spec = pl.BlockSpec((1, inner_rows, channels, samples), lambda s: (s, 0, 0, 0))
    middle, *packed = pl.pallas_call(
        inner_kernel,
        grid=(shots_here,),
        in_specs=[smem, smem, main_spec] + table_specs,
        out_specs=[middle_spec] + [anywhere] * CHUNKS,
        out_shape=[jax.ShapeDtypeStruct((shots_here, inner_rows, channels, samples), BF16)]
        + [packed_type] * CHUNKS,
        scratch_shapes=[
            pltpu.VMEM((tiles, channels * PITCH, LANES), F32),
            pltpu.VMEM((here, channels, samples), BF16),
            pltpu.VMEM((2, CHUNKS, here - 16, channels, LANES), BF16),
            pltpu.SemaphoreType.DMA((2,)),
        ],
        compiler_params=params,
        cost_estimate=pl.CostEstimate(
            flops=30 * 10**9, bytes_accessed=60 * 10**6, transcendentals=0
        ),
        name="shot_inner",
    )(inverse_rms, send, shot_feats, taps, weights, bias)
    packed = pl.pallas_call(
        edge_kernel,
        grid=(shots_here,),
        in_specs=[smem, smem, smem, main_spec, halo_spec, halo_spec, middle_spec]
        + table_specs
        + [anywhere] * CHUNKS,
        out_specs=[anywhere] * CHUNKS,
        out_shape=[packed_type] * CHUNKS,
        input_output_aliases={10 + i: i for i in range(CHUNKS)},
        scratch_shapes=[
            pltpu.VMEM((tiles, channels * PITCH, LANES), F32),
            pltpu.VMEM((4 * HALO, channels, samples), BF16),
            pltpu.VMEM((2, 16, channels, samples), BF16),
            pltpu.VMEM((2, CHUNKS, 16, channels, LANES), BF16),
            pltpu.SemaphoreType.DMA((2,)),
        ],
        compiler_params=params,
        name="shot_edges",
    )(inverse_rms, send, edges, shot_feats, low, high, middle, taps, weights, bias, *packed)

    buffers = [
        lax.all_to_all(
            part.reshape(blocks, capacity, channels, LANES),
            "shot",
            split_axis=0,
            concat_axis=0,
            tiled=True,
        ).reshape(slots, channels, LANES)
        for part in packed
    ]

    keep = jnp.maximum(recv_index.reshape(-1), 0)
    live_count = jnp.sum(recv_index >= 0, axis=1).astype(jnp.int32)
    recv_bias_rows = jnp.broadcast_to(recv_bias[:, :, None], recv_bias.shape + (samples,))
    return pl.pallas_call(
        recv_kernel,
        grid=(rows_here,),
        in_specs=[smem, smem] + table_specs + [anywhere] * CHUNKS,
        out_specs=pl.BlockSpec((channels, 1, fold, samples), lambda r: (0, r, 0, 0)),
        out_shape=jax.ShapeDtypeStruct((channels, rows_here, fold, samples), BF16),
        scratch_shapes=[
            pltpu.VMEM((2, CHUNKS, fold + 8, channels, LANES), BF16),
            pltpu.VMEM((fold + 8, channels, samples), BF16),
            pltpu.VMEM((tiles, channels * FOLDP, LANES), F32),
            pltpu.SemaphoreType.DMA((2,)),
        ],
        compiler_params=params,
        name="recv_domain",
    )(
        keep,
        live_count,
        tap_tables(recv_taps),
        mix_tables(recv_mix, recv_taps, None),
        recv_bias_rows,
        *buffers,
    )


def solution(mesh):
    return jax.shard_map(
        per_device,
        mesh=mesh,
        in_specs=(
            P(None, "shot", "recv", None),
            P(),
            P(),
            P(),
            P(),
            P(),
            P(),
            P(),
            P(("shot", "recv"), None),
            P(("shot", "recv"), None),
        ),
        out_specs=P(None, ("shot", "recv"), None, None),
        check_vma=False,
    )
```

time: 293 us -> 251 us (0.86)
  the two profiles are of different devices: /device:TPU:114 before, /device:TPU:0 now
where the time goes in v2:
time: 251 us; the launch traced here: 250 us
  blocking collectives  107 us (43%)
  Pallas kernels  80.8 us (32%)
  waiting for transfers between devices  38.8 us (15%)
  local copies, waits for them, and re-layouts  9.23 us (4%)
  starting transfers between devices  7.28 us (3%)
  other arithmetic  6.89 us (3%)
    all_to_all x2, blocking collectives, per_device(): lax.all_to_all(part.reshape(blocks, capacity, channels, LANES), 'shot', s...  92.5 us
    pallas_call x1, Pallas kernels, per_device(): pl.pallas_call(recv_kernel, grid=(rows_here,), in_specs=[smem, smem] + ta...  39.4 us
    all_to_all x1, waiting for transfers between devices, per_device(): lax.all_to_all(part.reshape(blocks, capacity, channels, LANES), 'shot', s...  38.8 us
    pallas_call x1, Pallas kernels, per_device(): pl.pallas_call(inner_kernel, grid=(shots_here,), in_specs=[smem, smem, ma...  23.2 us
    pallas_call x1, Pallas kernels, per_device(): pl.pallas_call(edge_kernel, grid=(shots_here,), in_specs=[smem, smem, sme...  18.3 us
    psum x1, blocking collectives, per_device(): lax.psum(jnp.sum(jnp.square(shot_feats.astype(F32)), axis=(0, 2, 3)), 're...  14.7 us
  transfers between devices with their start and end apart: 3, of which 1 were waited for; matrix products, arithmetic and copies ran while one was open for 3% of the time, Pallas kernels for 9%

profile of v2, /device:TPU:0, one launch (start us, length us, event | category | flops | bytes accessed | tf_op | source)
XLA Modules:
  0.0 250.5 jit_solution(9905357785037709785)
XLA Ops:
  0.0 0.0 copy-start.1
  0.0 4.7 %multiply_reduce_fusion = f32[4]{0:T(128)S(1)} fusion(bf16[64,4,32,384]{3,2,1,0:T(8,128)(2,1)} %main.3), kind=kLoop, calls=%fused_computation | loop fusion | flops 9437180 | bytes 6291472 | tf_op jit(solution)/shard_map/reduce_sum | solution.py:354
  4.7 0.0 copy-done.1
  4.7 0.0 copy-start.5
  4.7 0.0 copy-start.3
  4.7 2.0 fusion
  6.7 14.7 %psum.7 = f32[4]{0:T(128)S(1)} all-reduce(f32[4]{0:T(128)S(1)} %multiply_reduce_fusion), channel_id=1, replica_groups=mesh['shot'=16,'recv'=8] {'recv'}, use_global_device_ids=true, to_apply=%region_2.3 | all-reduce | flops 4 | bytes 32 | tf_op jit(solution)/shard_map/psum | solution.py:354
  21.4 1.4 collective-permute-start
  22.8 1.3 collective-permute-start.1
  24.1 0.0 copy-done.5
  24.1 0.1 mul.56
  24.2 0.0 copy-done.3
  24.2 0.1 copy.34
  24.4 0.8 copy.37
  25.2 0.7 stack.19
  25.8 0.1 mul.60
  25.9 0.8 eq.21
  26.7 0.1 select_reduce_fusion.send
  26.8 0.1 add_convert_fusion.edges
  26.9 0.9 multiply_convert_fusion.weights
  27.9 0.1 broadcast_in_dim.24.taps
  28.0 0.8 broadcast_in_dim.25.bias
  28.8 23.2 %shot_inner.1 = (bf16[4,24,64,384]{3,2,1,0:T(8,128)(2,1)}, bf16[192,64,128]{2,1,0:T(8,128)(2,1)S(1)}, bf16[192,64,128]{2,1,0:T(8,128)(2,1)}, bf16[192,64,128]{2,1,0:T(8,128)(2,1)}) custom-call(f32[4]{0:T(128)S(1)} %add_rsqrt_fusion.inverse_rms, s32[128]{0:T(128)S(1)} %select_reduce_fusion.send, bf16[64,4,32,384]{3,2,1,0:T(8,128)(2,1)} %main.3, ...), custom_call_target="tpu_custom_call" | custom-call | flops 30000001024 | bytes 60000000 | tf_op jit(solution)/shard_map/shot_inner/pallas_call | solution.py:390
  52.0 0.0 copy-start
  52.0 1.7 copy-done
  53.7 0.0 collective-permute-done.low
  53.7 0.0 collective-permute-done.1.high
  53.7 18.3 %shot_edges.1 = (bf16[192,64,128]{2,1,0:T(8,128)(2,1)}, bf16[192,64,128]{2,1,0:T(8,128)(2,1)}, bf16[192,64,128]{2,1,0:T(8,128)(2,1)}) custom-call(f32[4]{0:T(128)S(1)} %add_rsqrt_fusion.inverse_rms, s32[128]{0:T(128)S(1)} %select_reduce_fusion.send, s32[2]{0:T(128)S(1)} %add_convert_fusion.edges, ...), custom_call_target="tpu_custom_call", output_to_operand_aliasing={{0}: (10, {}), {1}: (11, {}), {2}: (12, {})} | custom-call | tf_op jit(solution)/shard_map/shot_edges/pallas_call | solution.py:409
  72.0 0.0 copy-start.2
  72.0 48.8 %all_to_all.15 = bf16[16,12,64,128]{3,2,1,0:T(8,128)(2,1)S(1)} all-to-all(bf16[16,12,64,128]{3,2,1,0:T(8,128)(2,1)} %bitcast.28), channel_id=1, replica_groups=mesh['shot'=16,'recv'=8] {'shot'}, dimensions={0} | all-to-all | bytes 6291456 | tf_op jit(solution)/shard_map/all_to_all | solution.py:430
  120.8 0.0 copy-done.2
  120.8 43.7 %all_to_all.16 = bf16[16,12,64,128]{3,2,1,0:T(8,128)(2,1)} all-to-all(bf16[16,12,64,128]{3,2,1,0:T(8,128)(2,1)S(1)} %bitcast.30), channel_id=1, replica_groups=mesh['shot'=16,'recv'=8] {'shot'}, dimensions={0} | all-to-all | bytes 6291456 | tf_op jit(solution)/shard_map/all_to_all | solution.py:430
  164.5 0.0 copy-start.6
  164.5 0.0 copy-start.4
  164.5 4.6 %all-to-all-start.2 = ((bf16[16,12,64,128]{3,2,1,0:T(8,128)(2,1)}), bf16[16,12,64,128]{3,2,1,0:T(8,128)(2,1)}, u32[]{:S(2)}, u32[]{:S(2)}) async-start(bf16[16,12,64,128]{3,2,1,0:T(8,128)(2,1)} %bitcast.31), calls=%async_computation.2 | async-start | bytes 6291456 | tf_op jit(solution)/shard_map/all_to_all | solution.py:430
  169.1 0.0 copy-done.6
  169.2 0.1 mul.51
  169.3 0.0 copy-done.4
  169.3 0.1 copy.28
  169.4 0.8 copy.31
  170.2 0.0 copy-done.7
  170.2 0.1 convert_reduce_fusion
  170.3 0.1 max.10.keep
  170.4 1.0 multiply_convert_fusion.1.weights
  171.4 38.8 %all-to-all-done.2 = bf16[16,12,64,128]{3,2,1,0:T(8,128)(2,1)} async-done(((bf16[16,12,64,128]{3,2,1,0:T(8,128)(2,1)}), bf16[16,12,64,128]{3,2,1,0:T(8,128)(2,1)}, u32[]{:S(2)}, u32[]{:S(2)}) %all-to-all-start.2) | async-done | bytes 3145760 | tf_op jit(solution)/shard_map/all_to_all | solution.py:430
  210.2 0.1 broadcast_in_dim.20.taps
  210.3 0.8 broadcast_in_dim.21.bias
  211.1 39.4 %recv_domain.1 = bf16[64,8,24,384]{3,2,1,0:T(8,128)(2,1)} custom-call(s32[192]{0:T(256)S(1)} %max.10.keep, s32[8]{0:T(128)S(1)} %get-tuple-element.31.live_count, f32[2,5,64,128]{3,2,1,0:T(8,128)S(1)} %broadcast_in_dim.20.taps, bf16[2,64,320]{2,1,0:T(8,128)(2,1)S(1)} %multiply_convert_fusion.1.weights, f32[2,64,384]{2,1,0:T(8,128)S(1)} %broadcast_in_dim.21.bias, ...), custom_call_target="tpu_custom_call" | custom-call | tf_op jit(solution)/shard_map/recv_domain/pallas_call | solution.py:443
  (13 shorter events, 0.1 us)
Async XLA Ops:
  0.0 4.7 %copy-start.1 = (bf16[64,4,32,384]{3,2,1,0:T(8,128)(2,1)S(1)}, bf16[64,4,32,384]{3,2,1,0:T(8,128)(2,1)}, u32[]{:S(2)}) copy-start(bf16[64,4,32,384]{3,2,1,0:T(8,128)(2,1)} %main.3) | copy-start | bytes 18874372
  4.7 19.4 %copy-start.5 = (f32[2,2,64,5]{2,1,3,0:T(2,128)S(1)}, f32[2,2,64,5]{2,1,3,0:T(2,128)}, u32[]{:S(2)}) copy-start(f32[2,2,64,5]{2,1,3,0:T(2,128)} %param.12) | copy-start | bytes 15364
  4.7 19.5 %copy-start.3 = (bf16[2,64,64]{2,1,0:T(8,128)(2,1)S(1)}, bf16[2,64,64]{2,1,0:T(8,128)(2,1)}, u32[]{:S(2)}) copy-start(bf16[2,64,64]{2,1,0:T(8,128)(2,1)} %param.13) | copy-start | bytes 49156
  21.4 32.3 %collective-permute-start = (bf16[64,4,8,384]{3,2,1,0:T(8,128)(2,1)}, bf16[64,4,8,384]{3,2,1,0:T(8,128)(2,1)S(1)}, u32[]{:S(2)}, u32[]{:S(2)}) collective-permute-start(bf16[64,4,8,384]{3,2,1,0:T(8,128)(2,1)} %get-tuple-element.16), channel_id=1, source_target_pairs={{0,1},{1,2},{2,3},{3,4},{4,5},{5,6},{6,7},{8,9},{9,10},{10,11},{11... | collective-permute-start | bytes 4718600 | tf_op jit(solution)/shard_map/ppermute | solution.py:358
  22.8 30.9 %collective-permute-start.1 = (bf16[64,4,8,384]{3,2,1,0:T(8,128)(2,1)}, bf16[64,4,8,384]{3,2,1,0:T(8,128)(2,1)S(1)}, u32[]{:S(2)}, u32[]{:S(2)}) collective-permute-start(bf16[64,4,8,384]{3,2,1,0:T(8,128)(2,1)} %get-tuple-element.17), channel_id=1, source_target_pairs={{1,0},{2,1},{3,2},{4,3},{5,4},{6,5},{7,6},{9,8},{10,9},{11,10},{12... | collective-permute-start | bytes 4718600 | tf_op jit(solution)/shard_map/ppermute | solution.py:359
  52.0 1.7 copy-start
  72.0 48.8 %copy-start.2 = (bf16[192,64,128]{2,1,0:T(8,128)(2,1)S(1)}, bf16[192,64,128]{2,1,0:T(8,128)(2,1)}, u32[]{:S(2)}) copy-start(bf16[192,64,128]{2,1,0:T(8,128)(2,1)} %get-tuple-element.23) | copy-start | bytes 9437188
  164.5 4.6 %copy-start.6 = (f32[2,2,64,5]{2,1,3,0:T(2,128)S(1)}, f32[2,2,64,5]{2,1,3,0:T(2,128)}, u32[]{:S(2)}) copy-start(f32[2,2,64,5]{2,1,3,0:T(2,128)} %param.15) | copy-start | bytes 15364
  164.5 4.8 %copy-start.4 = (bf16[2,64,64]{2,1,0:T(8,128)(2,1)S(1)}, bf16[2,64,64]{2,1,0:T(8,128)(2,1)}, u32[]{:S(2)}) copy-start(bf16[2,64,64]{2,1,0:T(8,128)(2,1)} %param.16) | copy-start | bytes 49156
  164.5 5.7 %copy-start.7 = (s32[8,24]{1,0:T(8,128)S(1)}, s32[8,24]{1,0:T(8,128)}, u32[]{:S(2)}) copy-start(s32[8,24]{1,0:T(8,128)} %param.19) | copy-start | bytes 2308
  164.5 45.7 %all-to-all-start.2 = ((bf16[16,12,64,128]{3,2,1,0:T(8,128)(2,1)}), bf16[16,12,64,128]{3,2,1,0:T(8,128)(2,1)}, u32[]{:S(2)}, u32[]{:S(2)}) async-start(bf16[16,12,64,128]{3,2,1,0:T(8,128)(2,1)} %bitcast.31), calls=%async_computation.2 | async-start | bytes 6291456 | tf_op jit(solution)/shard_map/all_to_all | solution.py:430

commit v3 on v2

--- a/solution.py
+++ b/solution.py
@@ -1,3 +1,5 @@
+import functools
+
 import jax
 import jax.numpy as jnp
 from jax import lax
@@ -216,19 +218,18 @@
         drain(staged, packed, sems, half)
 
 
-def recv_kernel(
-    keep,
-    live_count,
-    taps,
-    weights,
-    bias,
-    *rest,
-):
-    buffers, (out, gathered, middle, turned, sems) = rest[:CHUNKS], rest[CHUNKS:]
+def recv_kernel(first_call, keep, live_count, taps, weights, bias, *rest):
+    buffers, rest = rest[:2], rest[2:]
+    if first_call:
+        out, seam = rest[:2]
+    else:
+        seam, out = rest[0], rest[2]
+    gathered, middle, turned, sems = rest[-4:]
     row = pl.program_id(0)
     rows = pl.num_programs(0)
-    channels, _, fold, samples = out.shape
-    tiles = samples // LANES
+    channels, _, fold, _ = out.shape
+    tiles = len(buffers)
+    samples = tiles * LANES
     half = lax.rem(row, 2)
 
     def fetch(r, into):
@@ -236,7 +237,7 @@
             for q in range(4):
                 k = i * 4 + q
                 slot = keep[r * fold + k]
-                for j in range(CHUNKS):
+                for j in range(tiles):
                     pltpu.make_async_copy(
                         buffers[j].at[slot], gathered.at[into, j, 4 + k], sems.at[into]
                     ).start()
@@ -249,7 +250,7 @@
         fetch(0, 0)
         edge = jnp.zeros((4, channels, samples), BF16)
         for which in range(2):
-            for j in range(CHUNKS):
+            for j in range(tiles):
                 gathered[which, j, 0:4] = edge[:, :, :LANES]
                 gathered[which, j, fold + 4 : fold + 8] = edge[:, :, :LANES]
         middle[0:4] = edge
@@ -259,14 +260,14 @@
     def _():
         fetch(row + 1, 1 - half)
 
-    for j in range(CHUNKS):
+    for j in range(tiles):
         pltpu.make_async_copy(
             buffers[j].at[pl.ds(0, fold)], gathered.at[half, j, pl.ds(4, fold)], sems.at[half]
         ).wait()
     live = live_count[row]
 
     def clear(k, _):
-        for j in range(CHUNKS):
+        for j in range(tiles):
             gathered[half, j, 4 + k] = jnp.zeros((channels, LANES), BF16)
         return 0
 
@@ -277,7 +278,7 @@
         outs = group_linear(gathered.at[half], i * GROUP, taps.at[0], weights.at[0], GROUP)
         for q in range(GROUP):
             k = i * GROUP + q
-            value = jnp.maximum(outs[q] + bias[0], 0.0)
+            value = jnp.maximum(outs[q] + bias[0, :, :samples], 0.0)
             middle[4 + k] = jnp.where(k < live, value, 0.0).astype(BF16)
         return 0
 
@@ -295,19 +296,28 @@
         outs = group_linear(middle, i * GROUP, taps.at[1], weights.at[1], GROUP)
         for q in range(GROUP):
             k = i * GROUP + q
-            value = jnp.where(k < live, jnp.maximum(outs[q] + bias[1], 0.0), 0.0)
+            value = jnp.where(k < live, jnp.maximum(outs[q] + bias[1, :, :samples], 0.0), 0.0)
             for j in range(tiles):
                 turned[j, pl.ds(k, channels, stride=FOLDP), :] = value[:, j * LANES : (j + 1) * LANES]
         return 0
 
     lax.fori_loop(0, groups, second_layer, 0)
+
+    near = lax.broadcasted_iota(jnp.int32, (fold, LANES), 1) < LANES // 2
 
     def store_channel(i, _):
         for q in range(4):
             c = i * 4 + q
             base = c * FOLDP
-            for j in range(tiles):
-                out[c, 0, :, j * LANES : (j + 1) * LANES] = turned[j, pl.ds(base, fold), :].astype(BF16)
+            left = turned[0, pl.ds(base, fold), :]
+            right = turned[1, pl.ds(base, fold), :]
+            if first_call:
+                seam[c, 0] = left.astype(BF16)
+                out[c, 0] = right.astype(BF16)
+            else:
+                out[c, 0, :, :LANES] = left.astype(BF16)
+                joined = jnp.where(near, right, seam[c, 0].astype(F32))
+                out[c, 0, :, LANES:] = joined.astype(BF16)
         return 0
 
     lax.fori_loop(0, channels // 4, store_channel, 0)
@@ -426,42 +436,66 @@
         name="shot_edges",
     )(inverse_rms, send, edges, shot_feats, low, high, middle, taps, weights, bias, *packed)
 
-    buffers = [
-        lax.all_to_all(
+    def exchange(part):
+        return lax.all_to_all(
             part.reshape(blocks, capacity, channels, LANES),
             "shot",
             split_axis=0,
             concat_axis=0,
             tiled=True,
         ).reshape(slots, channels, LANES)
-        for part in packed
-    ]
+
+    third = exchange(packed[2])
+    second = exchange(packed[1])
+    second, third, waiting = lax.optimization_barrier((second, third, packed[0]))
+    first = exchange(waiting)
 
     keep = jnp.maximum(recv_index.reshape(-1), 0)
     live_count = jnp.sum(recv_index >= 0, axis=1).astype(jnp.int32)
-    recv_bias_rows = jnp.broadcast_to(recv_bias[:, :, None], recv_bias.shape + (samples,))
-    return pl.pallas_call(
-        recv_kernel,
-        grid=(rows_here,),
-        in_specs=[smem, smem] + table_specs + [anywhere] * CHUNKS,
-        out_specs=pl.BlockSpec((channels, 1, fold, samples), lambda r: (0, r, 0, 0)),
-        out_shape=jax.ShapeDtypeStruct((channels, rows_here, fold, samples), BF16),
-        scratch_shapes=[
-            pltpu.VMEM((2, CHUNKS, fold + 8, channels, LANES), BF16),
-            pltpu.VMEM((fold + 8, channels, samples), BF16),
-            pltpu.VMEM((tiles, channels * FOLDP, LANES), F32),
-            pltpu.SemaphoreType.DMA((2,)),
-        ],
-        compiler_params=params,
-        name="recv_domain",
-    )(
+    tables = (
         keep,
         live_count,
         tap_tables(recv_taps),
         mix_tables(recv_mix, recv_taps, None),
-        recv_bias_rows,
-        *buffers,
+        jnp.broadcast_to(recv_bias[:, :, None], recv_bias.shape + (samples,)),
     )
+    out_type = jax.ShapeDtypeStruct((channels, rows_here, fold, samples), BF16)
+    seam_type = jax.ShapeDtypeStruct((channels, rows_here, fold, LANES), BF16)
+
+    def lanes_spec(width, at):
+        return pl.BlockSpec((channels, 1, fold, width), lambda r: (0, r, 0, at))
+
+    scratch = [
+        pltpu.VMEM((2, 2, fold + 8, channels, LANES), BF16),
+        pltpu.VMEM((fold + 8, channels, 2 * LANES), BF16),
+        pltpu.VMEM((2, channels * FOLDP, LANES), F32),
+        pltpu.SemaphoreType.DMA((2,)),
+    ]
+    base_specs = [smem, smem] + table_specs + [anywhere] * 2
+    out, seam = pl.pallas_call(
+        functools.partial(recv_kernel, True),
+        grid=(rows_here,),
+        in_specs=base_specs,
+        out_specs=[lanes_spec(LANES, 2), lanes_spec(LANES, 0)],
+        out_shape=[out_type, seam_type],
+        scratch_shapes=scratch,
+        compiler_params=params,
+        cost_estimate=pl.CostEstimate(
+            flops=30 * 10**9, bytes_accessed=60 * 10**6, transcendentals=0
+        ),
+        name="recv_right",
+    )(*tables, second, third)
+    return pl.pallas_call(
+        functools.partial(recv_kernel, False),
+        grid=(rows_here,),
+        in_specs=base_specs + [lanes_spec(LANES, 0), anywhere],
+        out_specs=lanes_spec(2 * LANES, 0),
+        out_shape=out_type,
+        input_output_aliases={8: 0},
+        scratch_shapes=scratch,
+        compiler_params=params,
+        name="recv_left",
+    )(*tables, first, second, seam, out)
 
 
 def solution(mesh):

time: 251 us -> 257 us (1.024)
  blocking collectives: 107 us -> 63.8 us
  Pallas kernels: 80.8 us -> 103 us
  waiting for transfers between devices: 38.8 us -> 51 us
  starting transfers between devices: 7.28 us -> 15.5 us
  local copies, waits for them, and re-layouts: 9.23 us -> 14.1 us
    all_to_all x2 -> x1, blocking collectives: 92.5 us -> 48.6 us  [exchange(): lax.all_to_all(part.reshape(blocks, capacity, channels, LANES), 'shot', s...]
    pallas_call x1 -> x2, Pallas kernels: 39.4 us -> 61.5 us  [the longest x1 32.9 us: per_device(): pl.pallas_call(functools.partial(recv_kernel, False), grid=(rows_here,),...]
    all_to_all x1 -> x2, waiting for transfers between devices: 38.8 us -> 51 us  [exchange(): lax.all_to_all(part.reshape(blocks, capacity, channels, LANES), 'shot', s...]
    all_to_all x1 -> x2, starting transfers between devices: 4.61 us -> 12.8 us  [exchange(): lax.all_to_all(part.reshape(blocks, capacity, channels, LANES), 'shot', s...]
    unnamed x16 -> x36, local copies, waits for them, and re-layouts: 1.73 us -> 7.41 us
  transfers between devices with their start and end apart: 3 -> 4, of which waited for: 1 -> 2; matrix products, arithmetic and copies ran while one was open for 3% -> 3% of each run, Pallas kernels for 9% -> 20%
where the time goes in v3:
time: 257 us; the launch traced here: 255 us
  Pallas kernels  103 us (40%)
  blocking collectives  63.8 us (25%)
  waiting for transfers between devices  51 us (20%)
  starting transfers between devices  15.5 us (6%)
  local copies, waits for them, and re-layouts  14.1 us (5%)
  other arithmetic  6.6 us (3%)
    all_to_all x2, waiting for transfers between devices, exchange(): lax.all_to_all(part.reshape(blocks, capacity, channels, LANES), 'shot', s...  51 us
    all_to_all x1, blocking collectives, exchange(): lax.all_to_all(part.reshape(blocks, capacity, channels, LANES), 'shot', s...  48.6 us
    pallas_call x1, Pallas kernels, per_device(): pl.pallas_call(functools.partial(recv_kernel, False), grid=(rows_here,),...  32.9 us
    pallas_call x1, Pallas kernels, per_device(): pl.pallas_call(functools.partial(recv_kernel, True), grid=(rows_here,), i...  28.6 us
    pallas_call x1, Pallas kernels, per_device(): pl.pallas_call(inner_kernel, grid=(shots_here,), in_specs=[smem, smem, ma...  23.3 us
    pallas_call x1, Pallas kernels, per_device(): pl.pallas_call(edge_kernel, grid=(shots_here,), in_specs=[smem, smem, sme...  18.4 us
    psum x1, blocking collectives, per_device(): lax.psum(jnp.sum(jnp.square(shot_feats.astype(F32)), axis=(0, 2, 3)), 're...  15.2 us
    all_to_all x2, starting transfers between devices, exchange(): lax.all_to_all(part.reshape(blocks, capacity, channels, LANES), 'shot', s...  12.8 us
  transfers between devices with their start and end apart: 4, of which 2 were waited for; matrix products, arithmetic and copies ran while one was open for 3% of the time, Pallas kernels for 20%

profile of v3, /device:TPU:0, one launch (start us, length us, event | category | flops | bytes accessed | tf_op | source)
XLA Modules:
  0.0 254.5 jit_solution(15177512663816377988)
XLA Ops:
  0.0 4.7 %multiply_reduce_fusion = f32[4]{0:T(128)S(1)} fusion(bf16[64,4,32,384]{3,2,1,0:T(8,128)(2,1)} %main.3), kind=kLoop, calls=%fused_computation | loop fusion | flops 9437180 | bytes 6291472 | tf_op jit(solution)/shard_map/reduce_sum | solution.py:364
  4.7 0.0 copy-done.6
  4.7 0.0 copy-start.12
  4.7 0.0 copy-start.9
  4.7 2.1 fusion
  6.8 15.2 %psum.7 = f32[4]{0:T(128)} all-reduce(f32[4]{0:T(128)S(1)} %multiply_reduce_fusion), channel_id=1, replica_groups=mesh['shot'=16,'recv'=8] {'recv'}, use_global_device_ids=true, to_apply=%region_2.3 | all-reduce | flops 4 | bytes 32 | tf_op jit(solution)/shard_map/psum | solution.py:364
  22.0 1.4 collective-permute-start
  23.4 1.3 collective-permute-start.1
  24.7 0.0 copy-done.14
  24.7 0.1 eq.21
  24.8 0.1 select_reduce_fusion.send
  25.0 0.1 mul.60
  25.0 0.0 copy-done.12
  25.1 0.7 mul.56
  25.7 0.1 copy.35
  25.9 0.8 copy.38
  26.7 0.6 add_rsqrt_fusion.inverse_rms
  27.3 0.1 add_convert_fusion.edges
  27.4 1.0 multiply_convert_fusion.weights
  28.4 0.8 broadcast_in_dim.25.bias
  29.1 0.1 broadcast_in_dim.24.taps
  29.3 23.3 %shot_inner.1 = (bf16[4,24,64,384]{3,2,1,0:T(8,128)(2,1)}, bf16[192,64,128]{2,1,0:T(8,128)(2,1)S(1)}, bf16[192,64,128]{2,1,0:T(8,128)(2,1)}, bf16[192,64,128]{2,1,0:T(8,128)(2,1)}) custom-call(f32[4]{0:T(128)S(1)} %add_rsqrt_fusion.inverse_rms, s32[128]{0:T(128)S(1)} %select_reduce_fusion.send, bf16[64,4,32,384]{3,2,1,0:T(8,128)(2,1)} %main.3, ...), custom_call_target="tpu_custom_call" | custom-call | flops 30000001024 | bytes 60000000 | tf_op jit(solution)/shard_map/shot_inner/pallas_call | solution.py:400
  52.6 1.6 copy-done
  54.2 0.0 collective-permute-done.low
  54.2 0.0 collective-permute-done.1.high
  54.2 18.4 %shot_edges.1 = (bf16[192,64,128]{2,1,0:T(8,128)(2,1)}, bf16[192,64,128]{2,1,0:T(8,128)(2,1)}, bf16[192,64,128]{2,1,0:T(8,128)(2,1)}) custom-call(f32[4]{0:T(128)S(1)} %add_rsqrt_fusion.inverse_rms, s32[128]{0:T(128)S(1)} %select_reduce_fusion.send, s32[2]{0:T(128)S(1)} %add_convert_fusion.edges, ...), custom_call_target="tpu_custom_call", output_to_operand_aliasing={{0}: (10, {}), {1}: (11, {}), {2}: (12, {})} | custom-call | tf_op jit(solution)/shard_map/shot_edges/pallas_call | solution.py:419
  72.7 48.6 %all_to_all.15 = bf16[16,12,64,128]{3,2,1,0:T(8,128)(2,1)} all-to-all(bf16[16,12,64,128]{3,2,1,0:T(8,128)(2,1)} %bitcast.32), channel_id=1, replica_groups=mesh['shot'=16,'recv'=8] {'shot'}, dimensions={0} | all-to-all | bytes 6291456 | tf_op jit(solution)/shard_map/all_to_all | solution.py:440
  121.3 4.3 %all-to-all-start = ((bf16[16,12,64,128]{3,2,1,0:T(8,128)(2,1)}), bf16[16,12,64,128]{3,2,1,0:T(8,128)(2,1)S(1)}, u32[]{:S(2)}, u32[]{:S(2)}) async-start(bf16[16,12,64,128]{3,2,1,0:T(8,128)(2,1)} %bitcast.31), calls=%async_computation | async-start | bytes 6291456 | tf_op jit(solution)/shard_map/all_to_all | solution.py:440
  125.6 0.1 convert_reduce_fusion
  125.7 0.1 max.10.keep
  125.9 0.7 mul.51
  126.5 0.1 copy.29
  126.6 0.8 copy.32
  127.5 40.6 %all-to-all-done = bf16[16,12,64,128]{3,2,1,0:T(8,128)(2,1)S(1)} async-done(((bf16[16,12,64,128]{3,2,1,0:T(8,128)(2,1)}), bf16[16,12,64,128]{3,2,1,0:T(8,128)(2,1)S(1)}, u32[]{:S(2)}, u32[]{:S(2)}) %all-to-all-start) | async-done | bytes 3145760 | tf_op jit(solution)/shard_map/all_to_all | solution.py:440
  168.1 1.7 copy-done.7
  169.7 8.5 %all-to-all-start.2 = ((bf16[16,12,64,128]{3,2,1,0:T(8,128)(2,1)}), bf16[16,12,64,128]{3,2,1,0:T(8,128)(2,1)S(1)}, u32[]{:S(2)}, u32[]{:S(2)}) async-start(bf16[16,12,64,128]{3,2,1,0:T(8,128)(2,1)} %bitcast.28), calls=%async_computation.2 | async-start | bytes 6291456 | tf_op jit(solution)/shard_map/all_to_all | solution.py:440
  178.3 0.0 copy-start.4
  178.3 0.0 copy-done.16
  178.3 0.1 broadcast_in_dim.21.bias
  178.4 0.1 broadcast_in_dim.20.taps
  178.6 0.4 copy-done.4
  179.0 0.1 copy-done.2
  179.1 28.6 %recv_right.1 = (bf16[64,8,24,384]{3,2,1,0:T(8,128)(2,1)}, bf16[64,8,24,128]{3,2,1,0:T(8,128)(2,1)S(1)}) custom-call(s32[192]{0:T(256)S(1)} %max.10.keep, s32[8]{0:T(128)S(1)} %get-tuple-element.41.live_count, f32[2,5,64,128]{3,2,1,0:T(8,128)S(1)} %broadcast_in_dim.20.taps, bf16[2,64,320]{2,1,0:T(8,128)(2,1)S(1)} %multiply_convert_fusion.1.weights, ...), custom_call_target="tpu_custom_call" | custom-call | flops 30000001024 | bytes 60000000 | tf_op jit(solution)/shard_map/recv_right/pallas_call | solution.py:475
  207.7 1.7 copy-done.1
  209.4 10.4 %all-to-all-done.2 = bf16[16,12,64,128]{3,2,1,0:T(8,128)(2,1)S(1)} async-done(((bf16[16,12,64,128]{3,2,1,0:T(8,128)(2,1)}), bf16[16,12,64,128]{3,2,1,0:T(8,128)(2,1)S(1)}, u32[]{:S(2)}, u32[]{:S(2)}) %all-to-all-start.2) | async-done | bytes 3145760 | tf_op jit(solution)/shard_map/all_to_all | solution.py:440
  219.8 0.9 copy-done.3
  220.8 0.9 copy-done.5
  221.7 32.9 %recv_left.1 = bf16[64,8,24,384]{3,2,1,0:T(8,128)(2,1)} custom-call(s32[192]{0:T(256)S(1)} %max.10.keep, s32[8]{0:T(128)S(1)} %get-tuple-element.41.live_count, f32[2,5,64,128]{3,2,1,0:T(8,128)S(1)} %broadcast_in_dim.20.taps, bf16[2,64,320]{2,1,0:T(8,128)(2,1)S(1)} %copy-done.5, f32[2,64,384]{2,1,0:T(8,128)S(1)} %copy-done.3, ...), custom_call_target="tpu_custom_call", output_to_operand_aliasing={{}: (8, {})} | custom-call | tf_op jit(solution)/shard_map/recv_left/pallas_call | solution.py:488
  (35 shorter events, 0.2 us)
Async XLA Ops:
  0.0 4.7 %copy-start.6 = (bf16[64,4,32,384]{3,2,1,0:T(8,128)(2,1)S(1)}, bf16[64,4,32,384]{3,2,1,0:T(8,128)(2,1)}, u32[]{:S(2)}) copy-start(bf16[64,4,32,384]{3,2,1,0:T(8,128)(2,1)} %main.3) | copy-start | bytes 18874372
  4.7 20.0 %copy-start.14 = (s32[16,12]{1,0:T(8,128)S(1)}, s32[16,12]{1,0:T(8,128)}, u32[]{:S(2)}) copy-start(s32[16,12]{1,0:T(8,128)} %param.18) | copy-start | bytes 2308
  4.7 20.2 %copy-start.17 = (f32[64]{0:T(128)S(1)}, f32[64]{0:T(128)}, u32[]{:S(2)}) copy-start(f32[64]{0:T(128)} %param.11) | copy-start | bytes 772
  4.7 20.3 %copy-start.12 = (f32[2,2,64,5]{2,1,3,0:T(2,128)S(1)}, f32[2,2,64,5]{2,1,3,0:T(2,128)}, u32[]{:S(2)}) copy-start(f32[2,2,64,5]{2,1,3,0:T(2,128)} %param.12) | copy-start | bytes 15364
  4.7 21.0 %copy-start.9 = (bf16[2,64,64]{2,1,0:T(8,128)(2,1)S(1)}, bf16[2,64,64]{2,1,0:T(8,128)(2,1)}, u32[]{:S(2)}) copy-start(bf16[2,64,64]{2,1,0:T(8,128)(2,1)} %param.13) | copy-start | bytes 49156
  22.0 32.2 %collective-permute-start = (bf16[64,4,8,384]{3,2,1,0:T(8,128)(2,1)}, bf16[64,4,8,384]{3,2,1,0:T(8,128)(2,1)S(1)}, u32[]{:S(2)}, u32[]{:S(2)}) collective-permute-start(bf16[64,4,8,384]{3,2,1,0:T(8,128)(2,1)} %get-tuple-element.21), channel_id=1, source_target_pairs={{0,1},{1,2},{2,3},{3,4},{4,5},{5,6},{6,7},{8,9},{9,10},{10,11},{11... | collective-permute-start | bytes 4718600 | tf_op jit(solution)/shard_map/ppermute | solution.py:368
  23.4 30.8 %collective-permute-start.1 = (bf16[64,4,8,384]{3,2,1,0:T(8,128)(2,1)}, bf16[64,4,8,384]{3,2,1,0:T(8,128)(2,1)S(1)}, u32[]{:S(2)}, u32[]{:S(2)}) collective-permute-start(bf16[64,4,8,384]{3,2,1,0:T(8,128)(2,1)} %get-tuple-element.22), channel_id=1, source_target_pairs={{1,0},{2,1},{3,2},{4,3},{5,4},{6,5},{7,6},{9,8},{10,9},{11,10},{12... | collective-permute-start | bytes 4718600 | tf_op jit(solution)/shard_map/ppermute | solution.py:369
  52.6 1.7 copy-start
  121.3 4.3 %copy-start.15 = (s32[8,24]{1,0:T(8,128)S(1)}, s32[8,24]{1,0:T(8,128)}, u32[]{:S(2)}) copy-start(s32[8,24]{1,0:T(8,128)} %param.19) | copy-start | bytes 2308
  121.3 4.5 %copy-start.13 = (f32[2,2,64,5]{2,1,3,0:T(2,128)S(1)}, f32[2,2,64,5]{2,1,3,0:T(2,128)}, u32[]{:S(2)}) copy-start(f32[2,2,64,5]{2,1,3,0:T(2,128)} %param.15) | copy-start | bytes 15364
  121.3 5.2 %copy-start.10 = (bf16[2,64,64]{2,1,0:T(8,128)(2,1)S(1)}, bf16[2,64,64]{2,1,0:T(8,128)(2,1)}, u32[]{:S(2)}) copy-start(bf16[2,64,64]{2,1,0:T(8,128)(2,1)} %param.16) | copy-start | bytes 49156
  121.3 46.8 %all-to-all-start = ((bf16[16,12,64,128]{3,2,1,0:T(8,128)(2,1)}), bf16[16,12,64,128]{3,2,1,0:T(8,128)(2,1)S(1)}, u32[]{:S(2)}, u32[]{:S(2)}) async-start(bf16[16,12,64,128]{3,2,1,0:T(8,128)(2,1)} %bitcast.31), calls=%async_computation | async-start | bytes 6291456 | tf_op jit(solution)/shard_map/all_to_all | solution.py:440
  168.1 1.7 copy-start.7
  168.1 10.2 %copy-start.8 = (f32[2,64,320]{2,1,0:T(8,128)S(1)}, f32[2,64,320]{2,1,0:T(8,128)}, u32[]{:S(2)}) copy-start(f32[2,64,320]{2,1,0:T(8,128)} %copy.32) | copy-start | bytes 491524
  168.1 10.2 %copy-start.11 = (f32[2,320]{1,0:T(2,128)S(1)}, f32[2,320]{1,0:T(2,128)}, u32[]{:S(2)}) copy-start(f32[2,320]{1,0:T(2,128)} %mul.51) | copy-start | bytes 7684
  168.1 10.3 %copy-start.16 = (f32[2,64]{1,0:T(2,128)S(1)}, f32[2,64]{1,0:T(2,128)}, u32[]{:S(2)}) copy-start(f32[2,64]{1,0:T(2,128)} %param.17) | copy-start | bytes 1540
  169.7 50.1 %all-to-all-start.2 = ((bf16[16,12,64,128]{3,2,1,0:T(8,128)(2,1)}), bf16[16,12,64,128]{3,2,1,0:T(8,128)(2,1)S(1)}, u32[]{:S(2)}, u32[]{:S(2)}) async-start(bf16[16,12,64,128]{3,2,1,0:T(8,128)(2,1)} %bitcast.28), calls=%async_computation.2 | async-start | bytes 6291456 | tf_op jit(solution)/shard_map/all_to_all | solution.py:440
  178.3 0.6 copy-start.4
  178.4 0.7 copy-start.2
  207.7 1.7 copy-start.1
  219.8 0.9 copy-start.3
  220.8 0.9 copy-start.5

commit v4 on v2

--- a/solution.py
+++ b/solution.py
@@ -381,7 +381,7 @@
         whole(LAYERS, channels, 5 * channels),
         whole(LAYERS, channels, samples),
     ]
-    params = pltpu.CompilerParams(vmem_limit_bytes=48 * 2**20)
+    params = pltpu.CompilerParams(vmem_limit_bytes=58 * 2**20)
     tiles = samples // LANES
     inner_rows = here - 8
     main_spec = pl.BlockSpec((channels, 1, here, samples), lambda s: (0, s, 0, 0))

time: 251 us -> 247 us (0.984)
  Pallas kernels: 80.8 us -> 73.6 us
  other arithmetic: 6.89 us -> 10.4 us
    pallas_call x1, Pallas kernels: 39.4 us -> 35.2 us  [per_device(): pl.pallas_call(recv_kernel, grid=(rows_here,), in_specs=[smem, smem] + ta...]
  transfers between devices with their start and end apart: 3 -> 3, of which waited for: 1 -> 1; matrix products, arithmetic and copies ran while one was open for 3% -> 5% of each run, Pallas kernels for 9% -> 8%
where the time goes in v4:
time: 247 us; the launch traced here: 246 us
  blocking collectives  107 us (43%)
  Pallas kernels  73.6 us (30%)
  waiting for transfers between devices  37.5 us (15%)
  other arithmetic  10.4 us (4%)
  local copies, waits for them, and re-layouts  8.83 us (4%)
  starting transfers between devices  7.88 us (3%)
    all_to_all x2, blocking collectives, per_device(): lax.all_to_all(part.reshape(blocks, capacity, channels, LANES), 'shot', s...  92.5 us
    all_to_all x1, waiting for transfers between devices, per_device(): lax.all_to_all(part.reshape(blocks, capacity, channels, LANES), 'shot', s...  37.5 us
    pallas_call x1, Pallas kernels, per_device(): pl.pallas_call(recv_kernel, grid=(rows_here,), in_specs=[smem, smem] + ta...  35.2 us
    pallas_call x1, Pallas kernels, per_device(): pl.pallas_call(inner_kernel, grid=(shots_here,), in_specs=[smem, smem, ma...  20.8 us
    pallas_call x1, Pallas kernels, per_device(): pl.pallas_call(edge_kernel, grid=(shots_here,), in_specs=[smem, smem, sme...  17.6 us
    psum x1, blocking collectives, per_device(): lax.psum(jnp.sum(jnp.square(shot_feats.astype(F32)), axis=(0, 2, 3)), 're...  14.7 us
  transfers between devices with their start and end apart: 3, of which 1 were waited for; matrix products, arithmetic and copies ran while one was open for 5% of the time, Pallas kernels for 8%

profile of v4, /device:TPU:0, one launch (start us, length us, event | category | flops | bytes accessed | tf_op | source)
XLA Modules:
  0.0 245.6 jit_solution(8760965420844102224)
XLA Ops:
  0.0 0.0 copy-start
  0.0 4.7 %multiply_reduce_fusion = f32[4]{0:T(128)S(1)} fusion(bf16[64,4,32,384]{3,2,1,0:T(8,128)(2,1)} %main.3), kind=kLoop, calls=%fused_computation | loop fusion | flops 9437180 | bytes 6291472 | tf_op jit(solution)/shard_map/reduce_sum | solution.py:354
  4.7 0.0 copy-done
  4.7 0.0 copy-start.5
  4.7 0.0 copy-start.3
  4.7 0.0 copy-start.8
  4.7 0.4 fusion
  5.1 14.7 %psum.7 = f32[4]{0:T(128)S(1)} all-reduce(f32[4]{0:T(128)S(1)} %multiply_reduce_fusion), channel_id=1, replica_groups=mesh['shot'=16,'recv'=8] {'recv'}, use_global_device_ids=true, to_apply=%region_2.3 | all-reduce | flops 4 | bytes 32 | tf_op jit(solution)/shard_map/psum | solution.py:354
  19.8 2.4 collective-permute-start
  22.2 1.3 collective-permute-start.1
  23.5 0.6 add_rsqrt_fusion.inverse_rms
  24.1 0.0 copy-done.5
  24.1 0.1 mul.56
  24.2 0.0 copy-done.3
  24.2 0.1 copy.34
  24.3 0.8 copy.37
  25.2 0.7 stack.19
  25.8 0.1 mul.60
  25.9 0.8 eq.21
  26.7 0.6 select_reduce_fusion.send
  27.3 0.6 add_convert_fusion.edges
  28.0 1.6 multiply_convert_fusion.weights
  29.5 0.9 broadcast_in_dim.24.taps
  30.4 0.0 copy-done.8
  30.4 0.8 broadcast_in_dim.25.bias
  31.2 20.8 %shot_inner.1 = (bf16[4,24,64,384]{3,2,1,0:T(8,128)(2,1)}, bf16[192,64,128]{2,1,0:T(8,128)(2,1)}, bf16[192,64,128]{2,1,0:T(8,128)(2,1)}, bf16[192,64,128]{2,1,0:T(8,128)(2,1)}) custom-call(f32[4]{0:T(128)} %add_rsqrt_fusion.inverse_rms, s32[128]{0:T(128)} %select_reduce_fusion.send, bf16[64,4,32,384]{3,2,1,0:T(8,128)(2,1)} %main.3, ...), custom_call_target="tpu_custom_call" | custom-call | flops 30000001024 | bytes 60000000 | tf_op jit(solution)/shard_map/shot_inner/pallas_call | solution.py:390
  52.0 0.0 collective-permute-done.low
  52.0 0.0 collective-permute-done.1.high
  52.0 17.6 %shot_edges.1 = (bf16[192,64,128]{2,1,0:T(8,128)(2,1)}, bf16[192,64,128]{2,1,0:T(8,128)(2,1)}, bf16[192,64,128]{2,1,0:T(8,128)(2,1)}) custom-call(f32[4]{0:T(128)} %add_rsqrt_fusion.inverse_rms, s32[128]{0:T(128)} %select_reduce_fusion.send, s32[2]{0:T(128)} %add_convert_fusion.edges, ...), custom_call_target="tpu_custom_call", output_to_operand_aliasing={{0}: (10, {}), {1}: (11, {}), {2}: (12, {})} | custom-call | tf_op jit(solution)/shard_map/shot_edges/pallas_call | solution.py:409
  69.7 0.0 copy-start.2
  69.7 49.3 %all_to_all.15 = bf16[16,12,64,128]{3,2,1,0:T(8,128)(2,1)} all-to-all(bf16[16,12,64,128]{3,2,1,0:T(8,128)(2,1)} %bitcast.30), channel_id=1, replica_groups=mesh['shot'=16,'recv'=8] {'shot'}, dimensions={0} | all-to-all | bytes 6291456 | tf_op jit(solution)/shard_map/all_to_all | solution.py:430
  119.0 0.0 copy-done.2
  119.0 43.3 %all_to_all.16 = bf16[16,12,64,128]{3,2,1,0:T(8,128)(2,1)} all-to-all(bf16[16,12,64,128]{3,2,1,0:T(8,128)(2,1)S(1)} %bitcast.31), channel_id=1, replica_groups=mesh['shot'=16,'recv'=8] {'shot'}, dimensions={0} | all-to-all | bytes 6291456 | tf_op jit(solution)/shard_map/all_to_all | solution.py:430
  162.2 4.2 %all-to-all-start.2 = ((bf16[16,12,64,128]{3,2,1,0:T(8,128)(2,1)}), bf16[16,12,64,128]{3,2,1,0:T(8,128)(2,1)S(1)}, u32[]{:S(2)}, u32[]{:S(2)}) async-start(bf16[16,12,64,128]{3,2,1,0:T(8,128)(2,1)} %bitcast.32), calls=%async_computation.2 | async-start | bytes 6291456 | tf_op jit(solution)/shard_map/all_to_all | solution.py:430
  166.4 0.0 copy-done.6
  166.5 0.1 mul.51
  166.5 0.0 copy-done.4
  166.5 0.1 copy.28
  166.7 0.8 copy.31
  167.5 0.0 copy-done.7
  167.5 0.7 convert_reduce_fusion
  168.2 0.7 max.10.keep
  168.9 1.6 multiply_convert_fusion.1.weights
  170.4 37.5 %all-to-all-done.2 = bf16[16,12,64,128]{3,2,1,0:T(8,128)(2,1)S(1)} async-done(((bf16[16,12,64,128]{3,2,1,0:T(8,128)(2,1)}), bf16[16,12,64,128]{3,2,1,0:T(8,128)(2,1)S(1)}, u32[]{:S(2)}, u32[]{:S(2)}) %all-to-all-start.2) | async-done | bytes 3145760 | tf_op jit(solution)/shard_map/all_to_all | solution.py:430
  208.0 1.0 broadcast_in_dim.20.taps
  209.0 1.5 broadcast_in_dim.21.bias
  210.5 0.0 copy-done.1
  210.5 35.2 %recv_domain.1 = bf16[64,8,24,384]{3,2,1,0:T(8,128)(2,1)} custom-call(s32[192]{0:T(256)} %max.10.keep, s32[8]{0:T(128)} %get-tuple-element.31.live_count, f32[2,5,64,128]{3,2,1,0:T(8,128)} %broadcast_in_dim.20.taps, bf16[2,64,320]{2,1,0:T(8,128)(2,1)} %multiply_convert_fusion.1.weights, f32[2,64,384]{2,1,0:T(8,128)} %broadcast_in_dim.21.bias, ...), custom_call_target="tpu_custom_call" | custom-call | tf_op jit(solution)/shard_map/recv_domain/pallas_call | solution.py:443
  (15 shorter events, 0.1 us)
Async XLA Ops:
  0.0 4.7 %copy-start = (bf16[64,4,32,384]{3,2,1,0:T(8,128)(2,1)S(1)}, bf16[64,4,32,384]{3,2,1,0:T(8,128)(2,1)}, u32[]{:S(2)}) copy-start(bf16[64,4,32,384]{3,2,1,0:T(8,128)(2,1)} %main.3) | copy-start | bytes 18874372
  4.7 19.4 %copy-start.5 = (f32[2,2,64,5]{2,1,3,0:T(2,128)S(1)}, f32[2,2,64,5]{2,1,3,0:T(2,128)}, u32[]{:S(2)}) copy-start(f32[2,2,64,5]{2,1,3,0:T(2,128)} %param.12) | copy-start | bytes 15364
  4.7 19.5 %copy-start.3 = (bf16[2,64,64]{2,1,0:T(8,128)(2,1)S(1)}, bf16[2,64,64]{2,1,0:T(8,128)(2,1)}, u32[]{:S(2)}) copy-start(bf16[2,64,64]{2,1,0:T(8,128)(2,1)} %param.13) | copy-start | bytes 49156
  4.7 25.7 %copy-start.8 = (f32[2,64]{1,0:T(2,128)S(1)}, f32[2,64]{1,0:T(2,128)}, u32[]{:S(2)}) copy-start(f32[2,64]{1,0:T(2,128)} %param.14) | copy-start | bytes 1540
  19.8 32.3 %collective-permute-start = (bf16[64,4,8,384]{3,2,1,0:T(8,128)(2,1)S(1)}, bf16[64,4,8,384]{3,2,1,0:T(8,128)(2,1)}, u32[]{:S(2)}, u32[]{:S(2)}) collective-permute-start(bf16[64,4,8,384]{3,2,1,0:T(8,128)(2,1)S(1)} %get-tuple-element.16), channel_id=1, source_target_pairs={{0,1},{1,2},{2,3},{3,4},{4,5},{5,6},{6,7},{8,9},{9,10},{10,11},{11... | collective-permute-start | bytes 4718600 | tf_op jit(solution)/shard_map/ppermute | solution.py:358
  22.2 29.8 %collective-permute-start.1 = (bf16[64,4,8,384]{3,2,1,0:T(8,128)(2,1)S(1)}, bf16[64,4,8,384]{3,2,1,0:T(8,128)(2,1)}, u32[]{:S(2)}, u32[]{:S(2)}) collective-permute-start(bf16[64,4,8,384]{3,2,1,0:T(8,128)(2,1)S(1)} %get-tuple-element.17), channel_id=1, source_target_pairs={{1,0},{2,1},{3,2},{4,3},{5,4},{6,5},{7,6},{9,8},{10,9},{11,10},{12... | collective-permute-start | bytes 4718600 | tf_op jit(solution)/shard_map/ppermute | solution.py:359
  69.7 49.3 %copy-start.2 = (bf16[192,64,128]{2,1,0:T(8,128)(2,1)S(1)}, bf16[192,64,128]{2,1,0:T(8,128)(2,1)}, u32[]{:S(2)}) copy-start(bf16[192,64,128]{2,1,0:T(8,128)(2,1)} %get-tuple-element.23) | copy-start | bytes 9437188
  162.2 4.2 %copy-start.6 = (f32[2,2,64,5]{2,1,3,0:T(2,128)S(1)}, f32[2,2,64,5]{2,1,3,0:T(2,128)}, u32[]{:S(2)}) copy-start(f32[2,2,64,5]{2,1,3,0:T(2,128)} %param.15) | copy-start | bytes 15364
  162.2 4.3 %copy-start.4 = (bf16[2,64,64]{2,1,0:T(8,128)(2,1)S(1)}, bf16[2,64,64]{2,1,0:T(8,128)(2,1)}, u32[]{:S(2)}) copy-start(bf16[2,64,64]{2,1,0:T(8,128)(2,1)} %param.16) | copy-start | bytes 49156
  162.2 5.3 %copy-start.7 = (s32[8,24]{1,0:T(8,128)S(1)}, s32[8,24]{1,0:T(8,128)}, u32[]{:S(2)}) copy-start(s32[8,24]{1,0:T(8,128)} %param.19) | copy-start | bytes 2308
  162.2 45.7 %all-to-all-start.2 = ((bf16[16,12,64,128]{3,2,1,0:T(8,128)(2,1)}), bf16[16,12,64,128]{3,2,1,0:T(8,128)(2,1)S(1)}, u32[]{:S(2)}, u32[]{:S(2)}) async-start(bf16[16,12,64,128]{3,2,1,0:T(8,128)(2,1)} %bitcast.32), calls=%async_computation.2 | async-start | bytes 6291456 | tf_op jit(solution)/shard_map/all_to_all | solution.py:430
  208.0 2.5 %copy-start.1 = (bf16[16,12,64,128]{3,2,1,0:T(8,128)(2,1)}, bf16[16,12,64,128]{3,2,1,0:T(8,128)(2,1)S(1)}, u32[]{:S(2)}) copy-start(bf16[16,12,64,128]{3,2,1,0:T(8,128)(2,1)S(1)} %all-to-all-done.2) | copy-start | bytes 9437188
